TPU v7x, 32 devices: a whole 2x2x4 slice. The times are simulated.
32 devices in a mesh: groups: 2 (over y), expert: 8 (over z, x), tensor: 2 (over core).
Axes of the slice: x: 2, y: 2, z: 4, core: 2. Of those that a mesh axis runs over, the one named last changes fastest.
Arguments:
- tokens: bfloat16 [1024, 3584], P(('groups', 'expert')), parts along dimension 0, may hold values from -6 to 6
- expert_ids: int32 [1024, 2], P(('groups', 'expert')), parts along dimension 0, may hold values from 0 to 27, all different within a row; in each aligned block of 64 rows (0 to 63, 64 to 127, ...) at most 5 rows name the same one
- route_weights: float32 [1024, 2], P(('groups', 'expert')), parts along dimension 0, may hold values from 0.05 to 0.5
- slot_plan: int32 [64], P('groups'), parts along dimension 0, may hold values from 0 to 27, as said below
- w_gate: bfloat16 [256, 3584, 256], P(('groups', 'expert'), None, 'tensor'), parts along dimension 0, as said below
- w_up: bfloat16 [256, 3584, 256], P(('groups', 'expert'), None, 'tensor'), parts along dimension 0, as said below
- w_down: bfloat16 [256, 256, 3584], P(('groups', 'expert'), 'tensor'), parts along dimension 0, as said below
Outputs:
- mixed: bfloat16 [1024, 3584], P(('groups', 'expert'), 'tensor'), parts along dimension 0
There are 2 independent parts, one for each index of `groups`. A program takes and returns all parts, laid end to end along the dimension named above; each array names one. Nothing has to cross between parts.
Inputs may be any that keep to these rules, and one draw needn't show every extreme that they name: `expert_ids`: within the rows of one device (aligned blocks of 64 tokens) no expert is named more than 5 times; a token names 2 different experts. `slot_plan`: every expert is hosted by one slot, and exactly 4 experts by two. `w_gate`: slots that host the same expert hold equal blocks. `w_up`: slots that host the same expert hold equal blocks. `w_down`: slots that host the same expert hold equal blocks.
All inputs are finite; a program needn't handle non-finite values.
Results may differ from a plain program's by a relative error of at most 0.0065.
Values may be sent and summed in bfloat16 or wider, within the bound.
No kernel may reach another device: no remote copies, remote signals or barrier semaphores. Data moves between devices by JAX's collectives and lax.ppermute only.
A program may use at most 128 MiB of HBM per device.

v0:
```python
import jax
import jax.numpy as jnp
import numpy as np
from jax import lax
from jax.sharding import PartitionSpec as P

HB = 4
SLOTS = 32
EXPERTS = 28
CAP = 5


def swapped(shard, axis, stride):
    return lax.ppermute(shard, axis, [(i, i ^ 1 << stride) for i in range(lax.axis_size(axis))])


def shards(tokens, expert_ids, route_weights, slot_plan, w_gate, w_up, w_down):
    devices = lax.axis_size("expert")
    core = lax.axis_index("tensor")
    blocks_dev = w_gate.shape[0]
    slots_dev = max(1, blocks_dev // HB)
    width = tokens.shape[1]
    half = width // 2
    tok_rows = tokens.shape[0]
    picks_tok = expert_ids.shape[1]
    flat_ids = expert_ids.reshape(-1)
    slot_iota = jnp.arange(SLOTS, dtype=jnp.int32)
    expert_iota = jnp.arange(EXPERTS, dtype=jnp.int32)
    hosted = slot_plan[None, :] == expert_iota[:, None]
    first_slot = jnp.min(jnp.where(hosted, slot_iota[None, :], SLOTS), axis=1)
    naming = (flat_ids[:, None] == expert_iota[None, :]).astype(jnp.int32)
    lowest = jnp.sum(naming * first_slot[None, :], axis=1)
    placed = (lowest[:, None] == slot_iota[None, :]).astype(jnp.int32)
    position = jnp.sum((jnp.cumsum(placed, axis=0) - placed) * placed, axis=1)
    entry_iota = np.arange(devices * slots_dev)
    dest_slot = jnp.asarray(
        entry_iota // slots_dev * blocks_dev // HB + entry_iota % slots_dev, jnp.int32
    )
    slot_match = dest_slot[:, None] == lowest[None, :]
    row_match = jnp.arange(CAP, dtype=jnp.int32)[:, None] == position[None, :]
    routing = (slot_match[:, None, :] & row_match[None, :, :]).astype(jnp.int32)
    routing = routing.reshape(devices * slots_dev * CAP, tok_rows, picks_tok)
    tok_iota = jnp.arange(tok_rows, dtype=jnp.int32)
    source_row = jnp.sum(routing * tok_iota[None, :, None], axis=(1, 2))
    live_row = jnp.sum(routing, axis=(1, 2)) > 0
    block_slot = np.arange(blocks_dev) // HB
    outgoing = jnp.where(live_row[:, None], tokens[source_row], jnp.zeros((), jnp.bfloat16))
    outgoing = outgoing.reshape(devices, slots_dev, CAP, width)
    picked = jnp.take(
        lax.all_to_all(outgoing, "expert", split_axis=0, concat_axis=0, tiled=True),
        block_slot,
        axis=1,
    )
    gate = jnp.einsum("nbcd,bdu->nbcu", picked, w_gate, preferred_element_type=jnp.float32)
    upper = jnp.einsum("nbcd,bdu->nbcu", picked, w_up, preferred_element_type=jnp.float32)
    hidden = (jax.nn.silu(gate) * upper).astype(jnp.bfloat16)
    result = jnp.einsum("nbcu,bud->nbcd", hidden, w_down, preferred_element_type=jnp.float32)
    result = lax.optimization_barrier(result.astype(jnp.bfloat16))
    mine = lax.dynamic_slice_in_dim(result, core * half, half, 3)
    other = lax.dynamic_slice_in_dim(result, (1 - core) * half, half, 3)
    partner = swapped(other, "tensor", 0)
    outputs = (mine.astype(jnp.float32) + partner.astype(jnp.float32)).astype(jnp.bfloat16)
    returned = lax.all_to_all(outputs, "expert", split_axis=0, concat_axis=0, tiled=True)
    returned = returned.reshape(-1, half)
    block_iota = jnp.arange(HB, dtype=jnp.int32)
    row_index = (lowest[:, None] * HB + block_iota[None, :]) * CAP + position[:, None]
    gathered = returned[row_index.reshape(-1)].reshape(tok_rows, picks_tok, HB, half)
    summed = jnp.sum(gathered.astype(jnp.float32), axis=2)
    mixed = jnp.sum(summed * route_weights[:, :, None], axis=1)
    return mixed.astype(jnp.bfloat16)


def solution(mesh):
    in_specs = (
        P(("groups", "expert"), None),
        P(("groups", "expert"), None),
        P(("groups", "expert"), None),
        P("groups"),
        P(("groups", "expert"), None, "tensor"),
        P(("groups", "expert"), None, "tensor"),
        P(("groups", "expert"), "tensor", None),
    )
    out_specs = P(("groups", "expert"), "tensor")
    return jax.shard_map(shards, mesh=mesh, in_specs=in_specs, out_specs=out_specs, check_vma=False)
```

profile of v0, /device:TPU:0, one launch (start us, length us, event | category | flops | bytes accessed | tf_op | source)
XLA Modules:
  0.0 156.8 jit_solution(4797183254104972863)
XLA Ops:
  0.0 0.8 copy.40
  1.0 0.8 select_reduce_fusion.2
  2.5 0.3 fusion.34
  3.0 1.3 gather_fusion
  4.2 0.5 gather.13
  5.1 1.7 %copy.43 = bf16[8,4,5,3584]{3,1,2,0:T(4,128)(2,1)} copy(bf16[8,4,5,3584]{3,2,1,0:T(8,128)(2,1)S(1)} %broadcast_select_fusion) | data formatting | bytes 2293760 | tf_op jit(solution)/shard_map/jit(_where)/select_n | solution.py:47
  6.8 7.3 %all-to-all-start = ((bf16[8,4,5,3584]{3,1,2,0:T(4,128)(2,1)}), bf16[8,4,5,3584]{3,1,2,0:T(4,128)(2,1)S(1)}, u32[]{:S(2)}, u32[]{:S(2)}) async-start(bf16[8,4,5,3584]{3,1,2,0:T(4,128)(2,1)} %copy.43), calls=%async_computation | async-start | bytes 2293760 | tf_op jit(solution)/shard_map/all_to_all | solution.py:50
  14.0 27.9 %all-to-all-done = bf16[8,4,5,3584]{3,1,2,0:T(4,128)(2,1)S(1)} async-done(((bf16[8,4,5,3584]{3,1,2,0:T(4,128)(2,1)}), bf16[8,4,5,3584]{3,1,2,0:T(4,128)(2,1)S(1)}, u32[]{:S(2)}, u32[]{:S(2)}) %all-to-all-start) | async-done | bytes 1146912 | tf_op jit(solution)/shard_map/all_to_all | solution.py:50
  42.1 2.9 %gather_fusion.1 = bf16[16,8,5,3584]{3,1,2,0:T(8,128)(2,1)} fusion(bf16[8,4,5,3584]{3,0,2,1:T(8,128)(2,1)S(1)} %copy.44, s32[1024]{0:T(1024)S(1)} %pad_clamp_fusion.1), kind=kCustom, calls=%fused_computation.1 | custom fusion | bytes 9175104 | tf_op jit(solution)/shard_map/jit(_take)/gather | solution.py:49
  45.0 8.9 %fusion.14 = f32[8,16,5,128]{3,0,2,1:T(8,128)S(1)} fusion(bf16[16,3584,128]{2,1,0:T(8,128)(2,1)} %param.13, bf16[16,8,5,3584]{3,1,2,0:T(8,128)(2,1)} %gather_fusion.1), kind=kOutput, calls=%fused_computation.15 | convolution fusion | flops 587202560 | bytes 19595264 | tf_op jit(solution)/shard_map/nbcd,bdu->nbcu/dot_general | solution.py:54
  53.9 6.5 %fusion.29 = bf16[8,16,5,128]{3,0,2,1:T(8,128)(2,1)S(1)} fusion(bf16[16,3584,128]{2,1,0:T(8,128)(2,1)} %param.14, bf16[16,8,5,3584]{3,1,2,0:T(8,128)(2,1)S(1)} %copy-done.2, f32[8,16,5,128]{3,0,2,1:T(8,128)S(1)} %fusion.14), kind=kOutput, calls=%fused_computation.18 | convolution fusion | flops 587694080 | bytes 19759104 | tf_op jit(solution)/shard_map/nbcd,bdu->nbcu/dot_general | solution.py:55
  60.4 7.3 %fusion.9 = bf16[8,16,5,3584]{3,0,2,1:T(8,128)(2,1)S(1)} fusion(bf16[8,16,5,128]{3,0,2,1:T(8,128)(2,1)S(1)} %fusion.29, bf16[16,128,3584]{2,1,0:T(8,128)(2,1)} %param.15), kind=kOutput, calls=%fused_computation.10 | convolution fusion | flops 589496320 | bytes 19431424 | tf_op jit(solution)/shard_map/nbcu,bud->nbcd/dot_general | solution.py:57
  67.7 2.0 %copy-done.3 = bf16[8,16,5,3584]{3,0,2,1:T(8,128)(2,1)} copy-done((bf16[8,16,5,3584]{3,0,2,1:T(8,128)(2,1)}, bf16[8,16,5,3584]{3,0,2,1:T(8,128)(2,1)S(1)}, u32[]{:S(2)}) %copy-start.3) | copy-done | bytes 4587544
  70.0 4.6 %collective-permute-done = bf16[8,16,5,1792]{3,0,2,1:T(8,128)(2,1)} collective-permute-done((bf16[8,16,5,1792]{3,0,2,1:T(8,128)(2,1)S(1)}, bf16[8,16,5,1792]{3,0,2,1:T(8,128)(2,1)}, u32[]{:S(2)}, u32[]{:S(2)}) %collective-permute-start) | collective-permute-done | bytes 2293792 | tf_op jit(solution)/shard_map/ppermute | solution.py:14
  74.5 2.9 %add_convert_fusion = bf16[8,16,5,1792]{3,0,2,1:T(8,128)(2,1)S(1)} fusion(bf16[8,16,5,1792]{3,0,2,1:T(8,128)(2,1)} %collective-permute-done, bf16[8,16,5,3584]{3,0,2,1:T(8,128)(2,1)} %copy-done.3, s32[]{:T(128)S(6)} %select_n.49), kind=kLoop, calls=%fused_computation.13 | loop fusion | flops 4587520 | bytes 6881284 | tf_op jit(solution)/shard_map/convert_element_type | solution.py:62
  77.4 1.8 %copy.45 = bf16[8,16,5,1792]{3,1,2,0:T(8,128)(2,1)} copy(bf16[8,16,5,1792]{3,0,2,1:T(8,128)(2,1)S(1)} %add_convert_fusion) | data formatting | bytes 4587520 | tf_op jit(solution)/shard_map/convert_element_type | solution.py:62
  79.2 3.8 %all-to-all-start.1 = ((bf16[8,16,5,1792]{3,1,2,0:T(8,128)(2,1)}), bf16[8,16,5,1792]{3,1,2,0:T(8,128)(2,1)S(1)}, u32[]{:S(2)}, u32[]{:S(2)}) async-start(bf16[8,16,5,1792]{3,1,2,0:T(8,128)(2,1)} %copy.45), calls=%async_computation.1 | async-start | bytes 4587520 | tf_op jit(solution)/shard_map/all_to_all | solution.py:63
  83.3 52.4 %all-to-all-done.1 = bf16[8,16,5,1792]{3,1,2,0:T(8,128)(2,1)S(1)} async-done(((bf16[8,16,5,1792]{3,1,2,0:T(8,128)(2,1)}), bf16[8,16,5,1792]{3,1,2,0:T(8,128)(2,1)S(1)}, u32[]{:S(2)}, u32[]{:S(2)}) %all-to-all-start.1) | async-done | bytes 2293792 | tf_op jit(solution)/shard_map/all_to_all | solution.py:63
  135.8 2.7 %copy.46 = bf16[8,16,5,1792]{3,2,1,0:T(8,128)(2,1)} copy(bf16[8,16,5,1792]{3,1,2,0:T(8,128)(2,1)S(1)} %all-to-all-done.1) | data formatting | bytes 4587520 | tf_op jit(solution)/shard_map/all_to_all | solution.py:63
  138.5 4.0 %reshape.162 = bf16[640,1792]{1,0:T(8,128)(2,1)S(1)} reshape(bf16[8,16,5,1792]{3,2,1,0:T(8,128)(2,1)} %copy.46) | data formatting | bytes 4587520 | tf_op jit(solution)/shard_map/reshape | solution.py:64
  142.5 3.1 %gather_fusion.2 = bf16[512,1792]{1,0:T(8,128)(2,1)} fusion(bf16[640,1792]{1,0:T(8,128)(2,1)S(1)} %reshape.162, s32[1024]{0:T(1024)S(1)} %pad_clamp_fusion), kind=kCustom, calls=%fused_computation.2 | custom fusion | bytes 3672064 | tf_op jit(solution)/shard_map/gather | solution.py:67
  145.6 4.5 %reshape.163 = f32[64,2,4,1792]{3,2,1,0:T(4,128)} reshape(bf16[512,1792]{1,0:T(8,128)(2,1)} %gather_fusion.2) | data formatting | bytes 5505024 | tf_op jit(solution)/shard_map/convert_element_type | solution.py:68
  150.1 4.7 %reduce_sum.61 = f32[64,2,1792]{2,1,0:T(2,128)S(1)} reduce(f32[64,2,4,1792]{3,2,1,0:T(4,128)} %reshape.163, f32[]{:T(128)} %constant.56.clone.1), dimensions={2}, to_apply=%region_6.7 | reduce | flops 688128 | bytes 4587524 | tf_op jit(solution)/shard_map/reduce_sum | solution.py:68
  154.8 2.0 %multiply_reduce_fusion = bf16[64,1792]{1,0:T(8,128)(2,1)} fusion(f32[64,2,1792]{2,1,0:T(2,128)S(1)} %reduce_sum.61, f32[64,2]{1,0:T(8,128)S(1)} %copy.47), kind=kLoop, calls=%fused_computation.19 | loop fusion | flops 344064 | bytes 1147392 | tf_op jit(solution)/shard_map/reduce_sum | solution.py:69
  (37 shorter events, 2.1 us)
Async XLA Ops:
  0.0 2.9 %copy-start = (bf16[64,3584]{1,0:T(8,128)(2,1)S(1)}, bf16[64,3584]{1,0:T(8,128)(2,1)}, u32[]{:S(2)}) copy-start(bf16[64,3584]{1,0:T(8,128)(2,1)} %param.9) | copy-start | bytes 1376260
  4.7 9.3 %copy-start.5 = (s32[16]{0:T(128)S(1)}, s32[16]{0:T(128)}, u32[]{:S(2)}) copy-start(s32[16]{0:T(128)} %constant.66) | copy-start | bytes 196
  6.8 35.1 %all-to-all-start = ((bf16[8,4,5,3584]{3,1,2,0:T(4,128)(2,1)}), bf16[8,4,5,3584]{3,1,2,0:T(4,128)(2,1)S(1)}, u32[]{:S(2)}, u32[]{:S(2)}) async-start(bf16[8,4,5,3584]{3,1,2,0:T(4,128)(2,1)} %copy.43), calls=%async_computation | async-start | bytes 2293760 | tf_op jit(solution)/shard_map/all_to_all | solution.py:50
  45.0 8.9 %copy-start.2 = (bf16[16,8,5,3584]{3,1,2,0:T(8,128)(2,1)S(1)}, bf16[16,8,5,3584]{3,1,2,0:T(8,128)(2,1)}, u32[]{:S(2)}) copy-start(bf16[16,8,5,3584]{3,1,2,0:T(8,128)(2,1)} %gather_fusion.1) | copy-start | bytes 13762564
  67.7 2.1 %copy-start.3 = (bf16[8,16,5,3584]{3,0,2,1:T(8,128)(2,1)}, bf16[8,16,5,3584]{3,0,2,1:T(8,128)(2,1)S(1)}, u32[]{:S(2)}) copy-start(bf16[8,16,5,3584]{3,0,2,1:T(8,128)(2,1)S(1)} %fusion.9) | copy-start | bytes 13762564
  69.9 4.6 %collective-permute-start = (bf16[8,16,5,1792]{3,0,2,1:T(8,128)(2,1)S(1)}, bf16[8,16,5,1792]{3,0,2,1:T(8,128)(2,1)}, u32[]{:S(2)}, u32[]{:S(2)}) collective-permute-start(bf16[8,16,5,1792]{3,0,2,1:T(8,128)(2,1)S(1)} %constant_dynamic-slice_fusion), channel_id=1, source_target_pairs={{0,1},{1,0},{2,3},{3,2},{4,5},{5,4},{6,7},{7,6},{8,9},{9,8},{10,11... | collective-permute-start | bytes 6881288 | tf_op jit(solution)/shard_map/ppermute | solution.py:14
  77.4 5.8 %copy-start.4 = (f32[64,2]{0,1:T(2,128)S(1)}, f32[64,2]{0,1:T(2,128)}, u32[]{:S(2)}) copy-start(f32[64,2]{0,1:T(2,128)} %param.11) | copy-start | bytes 1540
  79.2 56.6 %all-to-all-start.1 = ((bf16[8,16,5,1792]{3,1,2,0:T(8,128)(2,1)}), bf16[8,16,5,1792]{3,1,2,0:T(8,128)(2,1)S(1)}, u32[]{:S(2)}, u32[]{:S(2)}) async-start(bf16[8,16,5,1792]{3,1,2,0:T(8,128)(2,1)} %copy.45), calls=%async_computation.1 | async-start | bytes 4587520 | tf_op jit(solution)/shard_map/all_to_all | solution.py:63
  142.5 14.3 %copy-start.1 = (bf16[64,3584]{1,0:T(8,128)(2,1)S(1)}, bf16[64,3584]{1,0:T(8,128)(2,1)}, u32[]{:S(2)}) copy-start(bf16[64,3584]{1,0:T(8,128)(2,1)} %param.9) | copy-start | bytes 1376260
where the time goes:
time: 157 us
  waiting for transfers between devices  84.8 us (54%)
  local copies, waits for them, and re-layouts  26.4 us (17%)
  matrix products  22.7 us (14%)
  other arithmetic  11.5 us (7%)
  starting transfers between devices  11.1 us (7%)
    all_to_all x1, waiting for transfers between devices, shards(): lax.all_to_all(outputs, 'expert', split_axis=0, concat_axis=0, tiled=True)  52.4 us
    all_to_all x1, waiting for transfers between devices, shards(): lax.all_to_all(outgoing, 'expert', split_axis=0, concat_axis=0, tiled=True)  27.9 us
    dot_general x1, matrix products, shards(): jnp.einsum('nbcd,bdu->nbcu', picked, w_gate, preferred_element_type=jnp.f...  8.89 us
    dot_general x1, matrix products, shards(): jnp.einsum('nbcu,bud->nbcd', hidden, w_down, preferred_element_type=jnp.f...  7.26 us
    all_to_all x1, starting transfers between devices, shards(): lax.all_to_all(outgoing, 'expert', split_axis=0, concat_axis=0, tiled=True)  7.25 us
    dot_general x1, matrix products, shards(): jnp.einsum('nbcd,bdu->nbcu', picked, w_up, preferred_element_type=jnp.flo...  6.53 us
    reduce_sum x1, other arithmetic, shards(): summed = jnp.sum(gathered.astype(jnp.float32), axis=2)  4.71 us
    ppermute x1, waiting for transfers between devices, swapped(): lax.ppermute(shard, axis, [(i, i ^ 1 << stride) for i in range(lax.axis_s...  4.55 us
  transfers between devices with their start and end apart: 3, of which 3 were waited for; matrix products, arithmetic and copies ran while one was open for 0% of the time, Pallas kernels for 0%

commit v1 on v0

--- a/solution.py
+++ b/solution.py
@@ -1,13 +1,18 @@
+import functools
 import jax
 import jax.numpy as jnp
 import numpy as np
 from jax import lax
+from jax.experimental import pallas as pl
+from jax.experimental.pallas import tpu as pltpu
 from jax.sharding import PartitionSpec as P
 
 HB = 4
 SLOTS = 32
 EXPERTS = 28
 CAP = 5
+STEP_BLOCKS = 2
+MIB = 1 << 20
 
 
 def swapped(shard, axis, stride):
@@ -70,6 +75,225 @@
     return mixed.astype(jnp.bfloat16)
 
 
+def quotient(values, divisor):
+    return lax.shift_right_logical(values * ((1 << 16) // divisor + 1), 16)
+
+
+def iota(shape, axis):
+    return lax.broadcasted_iota(jnp.int32, shape, axis)
+
+
+def column(row):
+    size = row.shape[1]
+    eye = iota((size, size), 0) == iota((size, size), 1)
+    return jnp.sum(jnp.where(eye, row, jnp.zeros((), row.dtype)), axis=1, keepdims=True)
+
+
+def onehot(mask):
+    return jnp.where(mask, 1.0, 0.0).astype(jnp.bfloat16)
+
+
+def dot(left, right, over=1):
+    dims = (((over,), (0,)), ((), ()))
+    return lax.dot_general(left, right, dims, preferred_element_type=jnp.float32)
+
+
+def pick_kernel(slots_dev, key_ref, ids_ref, plan_ref, tok_ref, pick_ref, *send_refs):
+    rounds = len(send_refs)
+    rows = slots_dev * CAP
+    packed = 2 * rows * rounds
+    tok_rows, width = tok_ref.shape
+    half = width // 2
+    slots = plan_ref.shape[1]
+    plan = plan_ref[...]
+    earlier = (column(plan) == plan) & (iota((slots, slots), 0) < iota((slots, slots), 1))
+    repeated = jnp.sum(jnp.where(earlier, 1, 0), axis=0, keepdims=True) > 0
+    served = jnp.where(repeated, -1, plan)
+
+    index = iota((packed, 1), 0)
+    part = quotient(index, rows)
+    entry = quotient(index, CAP)
+    rank = index - entry * CAP
+    slot = (key_ref[0] ^ lax.shift_right_logical(part, 1)) * slots_dev + entry - part * slots_dev
+    side = part & 1
+    chosen = jnp.where(iota((packed, slots), 1) == slot, served, 0)
+    expert = jnp.sum(chosen, axis=1, keepdims=True)
+
+    ids = jnp.concatenate([ids_ref[...], ids_ref[...]], axis=1)
+    lanes = 2 * tok_rows
+    lane = iota((packed, lanes), 1)
+    same_side = jnp.where(lane < tok_rows, 0, 1) == side
+    named = [(expert == ids[k : k + 1, :]) & same_side for k in range(ids.shape[0])]
+    either = functools.reduce(jnp.logical_or, named)
+    before = onehot(iota((lanes, lanes), 0) < iota((lanes, lanes), 1))
+    in_row = dot(onehot(either), before) == rank.astype(jnp.float32)
+    for k, mask in enumerate(named):
+        pick_ref[k, :, :] = onehot(mask & in_row)
+    stacked = jnp.concatenate([tok_ref[:, :half], tok_ref[:, half:]], axis=0)
+    sent = dot(onehot(either & in_row), stacked).astype(jnp.bfloat16)
+    for p, send_ref in enumerate(send_refs):
+        send_ref[...] = sent[2 * rows * p : 2 * rows * (p + 1), :]
+
+
+def expert_kernel(slots_dev, bufs, *refs):
+    buf_refs = refs[:bufs]
+    gate_ref, up_ref, down_ref, mine_ref, other_ref, x_ref, acc_ref = refs[bufs:]
+    rows = slots_dev * CAP
+    total = bufs * rows
+    half = buf_refs[0].shape[1]
+    step = pl.program_id(0)
+
+    @pl.when(step == 0)
+    def _():
+        got = jnp.concatenate([ref[...] for ref in buf_refs], axis=0)
+        place = iota((total, 2 * total), 0)
+        place = place + rows * quotient(place, rows)
+        lane = iota((total, 2 * total), 1)
+        x_ref[:, :half] = dot(onehot(lane == place), got).astype(jnp.bfloat16)
+        x_ref[:, half:] = dot(onehot(lane == place + rows), got).astype(jnp.bfloat16)
+        acc_ref[...] = jnp.zeros_like(acc_ref)
+
+    x = x_ref[...]
+    index = iota((total, 1), 0)
+    row_slot = quotient(index, CAP) - quotient(index, rows) * slots_dev
+    hidden = []
+    for b in range(STEP_BLOCKS):
+        both = dot(x, jnp.concatenate([gate_ref[b], up_ref[b]], axis=1))
+        unit = gate_ref.shape[2]
+        gate, upper = both[:, :unit], both[:, unit:]
+        value = gate / (1.0 + jnp.exp(-gate)) * upper
+        mine = row_slot == (step * STEP_BLOCKS + b) // HB
+        hidden.append(jnp.where(mine, value, 0.0).astype(jnp.bfloat16))
+    down = jnp.concatenate([down_ref[b] for b in range(STEP_BLOCKS)], axis=0)
+    acc_ref[...] += dot(jnp.concatenate(hidden, axis=1), down)
+
+    @pl.when(step == pl.num_programs(0) - 1)
+    def _():
+        mine_ref[...] = acc_ref[: total // 2, :]
+        other_ref[...] = acc_ref[total // 2 :, :].astype(jnp.bfloat16)
+
+
+def sum_kernel(rows, mine_ref, got_ref, *send_refs):
+    total = mine_ref.shape[0]
+    half = mine_ref.shape[1] // 2
+    summed = (mine_ref[...] + got_ref[...].astype(jnp.float32)).astype(jnp.bfloat16)
+    stacked = jnp.concatenate([summed[:, :half], summed[:, half:]], axis=0)
+    index = iota((2 * total, 2 * total), 0)
+    part = quotient(index, rows)
+    source = index - rows * part + rows * lax.shift_right_logical(part, 1) + total * (part & 1)
+    packed = dot(onehot(iota((2 * total, 2 * total), 1) == source), stacked).astype(jnp.bfloat16)
+    for p, send_ref in enumerate(send_refs):
+        send_ref[...] = packed[2 * rows * p : 2 * rows * (p + 1), :]
+
+
+def combine_kernel(bufs, core_ref, pick_ref, weight_ref, *refs):
+    got = jnp.concatenate([ref[...] for ref in refs[:bufs]], axis=0)
+    keep_ref, give_ref, sum_ref = refs[bufs:]
+    tok_rows = keep_ref.shape[0]
+    mixed = None
+    for k in range(pick_ref.shape[0]):
+        weight = column(weight_ref[k : k + 1, :])
+        term = dot(pick_ref[k], got, 0) * jnp.concatenate([weight, weight], axis=0)
+        mixed = term if mixed is None else mixed + term
+    sum_ref[...] = mixed
+    core = core_ref[0]
+    keep_ref[...] = sum_ref[pl.ds(pl.multiple_of(core * tok_rows, 8), tok_rows), :]
+    give_ref[...] = sum_ref[pl.ds(pl.multiple_of((1 - core) * tok_rows, 8), tok_rows), :].astype(jnp.bfloat16)
+
+
+VMEM = pl.BlockSpec(memory_space=pltpu.VMEM)
+SMEM = pl.BlockSpec(memory_space=pltpu.SMEM)
+
+
+def params(mib):
+    return pltpu.CompilerParams(vmem_limit_bytes=mib * MIB)
+
+
+def shards_paired(tokens, expert_ids, route_weights, slot_plan, w_gate, w_up, w_down):
+    chips = lax.axis_size("expert")
+    rounds = chips // 2
+    core = lax.axis_index("tensor").astype(jnp.int32)
+    chip = lax.axis_index("expert").astype(jnp.int32)
+    slots_dev = w_gate.shape[0] // HB
+    rows = slots_dev * CAP
+    tok_rows, width = tokens.shape
+    half = width // 2
+    picks = expert_ids.shape[1]
+    packed = jax.ShapeDtypeStruct((2 * rows, half), jnp.bfloat16)
+    key = (chip ^ (core * rounds)).reshape(1)
+
+    def travel(arrays):
+        return [
+            lax.ppermute(
+                array,
+                ("expert", "tensor"),
+                [(2 * i + c, 2 * (i ^ (p + rounds * c)) + c) for i in range(chips) for c in range(2)],
+            )
+            for p, array in enumerate(arrays)
+        ]
+
+    pick, *sent = pl.pallas_call(
+        functools.partial(pick_kernel, slots_dev),
+        out_shape=[jax.ShapeDtypeStruct((picks, 2 * rows * rounds, 2 * tok_rows), jnp.bfloat16)] + [packed] * rounds,
+        in_specs=[SMEM, VMEM, VMEM, VMEM],
+        out_specs=[VMEM] * (1 + rounds),
+        compiler_params=params(16),
+        name="pick_rows",
+    )(key, expert_ids.T, slot_plan.reshape(1, -1), tokens)
+
+    got = travel(sent)
+    got = got + [swapped(array, "tensor", 0) for array in got]
+
+    total = chips * rows
+    blocks, _, unit = w_gate.shape
+    whole = lambda shape: pl.BlockSpec(shape, lambda i: (0, 0))
+    mine, other = pl.pallas_call(
+        functools.partial(expert_kernel, slots_dev, chips),
+        grid=(blocks // STEP_BLOCKS,),
+        out_shape=[
+            jax.ShapeDtypeStruct((total // 2, width), jnp.float32),
+            jax.ShapeDtypeStruct((total // 2, width), jnp.bfloat16),
+        ],
+        in_specs=[whole((2 * rows, half))] * chips
+        + [
+            pl.BlockSpec((STEP_BLOCKS, width, unit), lambda i: (i, 0, 0)),
+            pl.BlockSpec((STEP_BLOCKS, width, unit), lambda i: (i, 0, 0)),
+            pl.BlockSpec((STEP_BLOCKS, unit, width), lambda i: (i, 0, 0)),
+        ],
+        out_specs=[whole((total // 2, width))] * 2,
+        scratch_shapes=[
+            pltpu.VMEM((total, width), jnp.bfloat16),
+            pltpu.VMEM((total, width), jnp.float32),
+        ],
+        compiler_params=params(40),
+        name="experts",
+    )(*got, w_gate, w_up, w_down)
+
+    back = pl.pallas_call(
+        functools.partial(sum_kernel, rows),
+        out_shape=[packed] * rounds,
+        in_specs=[VMEM, VMEM],
+        out_specs=[VMEM] * rounds,
+        compiler_params=params(16),
+        name="sum_cores",
+    )(mine, swapped(other, "tensor", 0))
+
+    home = travel(back)
+    keep, give = pl.pallas_call(
+        functools.partial(combine_kernel, rounds),
+        out_shape=[
+            jax.ShapeDtypeStruct((tok_rows, half), jnp.float32),
+            jax.ShapeDtypeStruct((tok_rows, half), jnp.bfloat16),
+        ],
+        in_specs=[SMEM] + [VMEM] * (2 + rounds),
+        out_specs=[VMEM] * 2,
+        scratch_shapes=[pltpu.VMEM((2 * tok_rows, half), jnp.float32)],
+        compiler_params=params(16),
+        name="combine",
+    )(core.reshape(1), pick, route_weights.T, *home)
+    return (keep + swapped(give, "tensor", 0).astype(jnp.float32)).astype(jnp.bfloat16)
+
+
 def solution(mesh):
     in_specs = (
         P(("groups", "expert"), None),
@@ -81,4 +305,7 @@
         P(("groups", "expert"), "tensor", None),
     )
     out_specs = P(("groups", "expert"), "tensor")
-    return jax.shard_map(shards, mesh=mesh, in_specs=in_specs, out_specs=out_specs, check_vma=False)
+    chips = mesh.shape["expert"]
+    paired = mesh.shape["tensor"] == 2 and chips in (2, 4, 8) and SLOTS % chips == 0
+    body = shards_paired if paired else shards
+    return jax.shard_map(body, mesh=mesh, in_specs=in_specs, out_specs=out_specs, check_vma=False)

time: 157 us -> 63.1 us (0.40)
  waiting for transfers between devices: 84.8 us -> 9.55 us
  local copies, waits for them, and re-layouts: 26.4 us -> 2.35 us
  matrix products: 22.7 us -> 0 us
  Pallas kernels: 0 us -> 19.9 us
  starting transfers between devices: 11.1 us -> 29.7 us
  other arithmetic: 11.5 us -> 0.74 us
    all_to_all x2 -> x0, waiting for transfers between devices: 80.3 us -> none  [the longest x1 52.4 us: shards(): lax.all_to_all(outputs, 'expert', split_axis=0, concat_axis=0, tiled=True)]
    dot_general x3 -> x0, matrix products: 22.7 us -> none  [the longest x1 8.89 us: shards(): jnp.einsum('nbcd,bdu->nbcu', picked, w_gate, preferred_element_type=jnp.f...]
    pallas_call x0 -> x4, Pallas kernels: none -> 19.9 us  [the longest x1 18.4 us: shards_paired(): pl.pallas_call(functools.partial(expert_kernel, slots_dev, chips), grid=(...]
    ppermute x1 -> x6, starting transfers between devices: 0.07 us -> 19.6 us  [swapped(): lax.ppermute(shard, axis, [(i, i ^ 1 << stride) for i in range(lax.axis_s...]
    all_to_all x2 -> x0, starting transfers between devices: 11 us -> none  [the longest x1 7.25 us: shards(): lax.all_to_all(outgoing, 'expert', split_axis=0, concat_axis=0, tiled=True)]
    ppermute x0 -> x8, starting transfers between devices: none -> 10.1 us  [travel(): lax.ppermute(array, ('expert', 'tensor'), [(2 * i + c, 2 * (i ^ p + round...]
    gather x4 -> x0, local copies, waits for them, and re-layouts: 7.81 us -> none  [the longest x1 3.15 us: shards(): returned[row_index.reshape(-1)].reshape(tok_rows, picks_tok, HB, half)]
    reduce_sum x5 -> x0, other arithmetic: 7.18 us -> none  [the longest x1 4.71 us: shards(): summed = jnp.sum(gathered.astype(jnp.float32), axis=2)]
  transfers between devices with their start and end apart: 3 -> 14, of which waited for: 3 -> 6; matrix products, arithmetic and copies ran while one was open for 0% -> 0% of each run, Pallas kernels for 0% -> 0%
where the time goes in v1:
time: 63.1 us; the launch traced here: 62.3 us
  starting transfers between devices  29.7 us (47%)
  Pallas kernels  19.9 us (32%)
  waiting for transfers between devices  9.55 us (15%)
  local copies, waits for them, and re-layouts  2.35 us (4%)
  other arithmetic  0.74 us (1%)
    ppermute x6, starting transfers between devices, swapped(): lax.ppermute(shard, axis, [(i, i ^ 1 << stride) for i in range(lax.axis_s...  19.6 us
    pallas_call x1, Pallas kernels, shards_paired(): pl.pallas_call(functools.partial(expert_kernel, slots_dev, chips), grid=(...  18.4 us
    ppermute x8, starting transfers between devices, travel(): lax.ppermute(array, ('expert', 'tensor'), [(2 * i + c, 2 * (i ^ p + round...  10.1 us
    ppermute x8, waiting for transfers between devices, travel(): lax.ppermute(array, ('expert', 'tensor'), [(2 * i + c, 2 * (i ^ p + round...  5.81 us
    ppermute x6, waiting for transfers between devices, swapped(): lax.ppermute(shard, axis, [(i, i ^ 1 << stride) for i in range(lax.axis_s...  3.74 us
    unnamed x8, local copies, waits for them, and re-layouts  2.35 us
  transfers between devices with their start and end apart: 14, of which 6 were waited for; matrix products, arithmetic and copies ran while one was open for 0% of the time, Pallas kernels for 0%

profile of v1, /device:TPU:0, one launch (start us, length us, event | category | flops | bytes accessed | tf_op | source)
XLA Modules:
  0.0 62.3 jit_solution(14635904440952731861)
XLA Ops:
  0.0 1.0 %copy-done = bf16[64,3584]{1,0:T(8,128)(2,1)S(1)} copy-done((bf16[64,3584]{1,0:T(8,128)(2,1)S(1)}, bf16[64,3584]{1,0:T(8,128)(2,1)}, u32[]{:S(2)}) %copy-start) | copy-done | bytes 458776
  1.0 0.7 %copy-done.1 = s32[64,2]{0,1:T(2,128)S(1)} copy-done((s32[64,2]{0,1:T(2,128)S(1)}, s32[64,2]{0,1:T(2,128)}, u32[]{:S(2)}) %copy-start.1) | copy-done | bytes 536
  1.7 0.7 %copy-done.3 = s32[32]{0:T(128)S(1)} copy-done((s32[32]{0:T(128)S(1)}, s32[32]{0:T(128)}, u32[]{:S(2)}) %copy-start.3) | copy-done | bytes 152
  2.4 0.6 %pick_rows.1 = (bf16[2,160,128]{2,1,0:T(8,128)(2,1)S(1)}, bf16[40,1792]{1,0:T(8,128)(2,1)S(1)}, bf16[40,1792]{1,0:T(8,128)(2,1)S(1)}, bf16[40,1792]{1,0:T(8,128)(2,1)S(1)}, bf16[40,1792]{1,0:T(8,128)(2,1)S(1)}) custom-call(s32[1]{0:T(128)} %bitcast.1.key_ref, s32[2,64]{1,0:T(2,128)S(1)} %bitcast.5, s32[1,32]{1,0:T(1,128)S(1)} %bitcast.7, ...), custom_call_target="tpu_custom_call" | custom-call | tf_op jit(solution)/shard_map/pick_rows/pallas_call | solution.py:235
  3.0 0.7 %collective-permute-start = (bf16[40,1792]{1,0:T(8,128)(2,1)S(1)}, bf16[40,1792]{1,0:T(8,128)(2,1)S(1)}, u32[]{:S(2)}, u32[]{:S(2)}) collective-permute-start(bf16[40,1792]{1,0:T(8,128)(2,1)S(1)} %get-tuple-element.19), channel_id=1, source_target_pairs={{0,0},{1,9},{2,2},{3,11},{4,4},{5,13},{6,6},{7,15},{8,8},{9,1},{10... | collective-permute-start | bytes 430088 | tf_op jit(solution)/shard_map/ppermute | solution.py:227
  3.7 3.0 %collective-permute-start.1 = (bf16[40,1792]{1,0:T(8,128)(2,1)S(1)}, bf16[40,1792]{1,0:T(8,128)(2,1)S(1)}, u32[]{:S(2)}, u32[]{:S(2)}) collective-permute-start(bf16[40,1792]{1,0:T(8,128)(2,1)S(1)} %get-tuple-element.20), channel_id=1, source_target_pairs={{0,2},{1,11},{2,0},{3,9},{4,6},{5,15},{6,4},{7,13},{8,10},{9,3},{1... | collective-permute-start | bytes 430088 | tf_op jit(solution)/shard_map/ppermute | solution.py:227
  6.7 1.6 %collective-permute-start.2 = (bf16[40,1792]{1,0:T(8,128)(2,1)S(1)}, bf16[40,1792]{1,0:T(8,128)(2,1)S(1)}, u32[]{:S(2)}, u32[]{:S(2)}) collective-permute-start(bf16[40,1792]{1,0:T(8,128)(2,1)S(1)} %get-tuple-element.21), channel_id=1, source_target_pairs={{0,4},{1,13},{2,6},{3,15},{4,0},{5,9},{6,2},{7,11},{8,12},{9,5},{1... | collective-permute-start | bytes 430088 | tf_op jit(solution)/shard_map/ppermute | solution.py:227
  8.3 4.7 %collective-permute-start.4 = (bf16[40,1792]{1,0:T(8,128)(2,1)S(1)}, bf16[40,1792]{1,0:T(8,128)(2,1)S(1)}, u32[]{:S(2)}, u32[]{:S(2)}) collective-permute-start(bf16[40,1792]{1,0:T(8,128)(2,1)S(1)} %collective-permute-done.refs_0_), channel_id=1, source_target_pairs={{0,1},{1,0},{2,3},{3,2},{4,5},{5,4},{6,7},{7,6},{8,9},{9,8},{10,11... | collective-permute-start | bytes 430088 | tf_op jit(solution)/shard_map/ppermute | solution.py:19
  13.0 3.3 %collective-permute-start.5 = (bf16[40,1792]{1,0:T(8,128)(2,1)S(1)}, bf16[40,1792]{1,0:T(8,128)(2,1)S(1)}, u32[]{:S(2)}, u32[]{:S(2)}) collective-permute-start(bf16[40,1792]{1,0:T(8,128)(2,1)S(1)} %collective-permute-done.1.refs_1_), channel_id=1, source_target_pairs={{0,1},{1,0},{2,3},{3,2},{4,5},{5,4},{6,7},{7,6},{8,9},{9,8},{10,11... | collective-permute-start | bytes 430088 | tf_op jit(solution)/shard_map/ppermute | solution.py:19
  16.2 2.1 %collective-permute-start.6 = (bf16[40,1792]{1,0:T(8,128)(2,1)S(1)}, bf16[40,1792]{1,0:T(8,128)(2,1)S(1)}, u32[]{:S(2)}, u32[]{:S(2)}) collective-permute-start(bf16[40,1792]{1,0:T(8,128)(2,1)S(1)} %collective-permute-done.2.refs_2_), channel_id=1, source_target_pairs={{0,1},{1,0},{2,3},{3,2},{4,5},{5,4},{6,7},{7,6},{8,9},{9,8},{10,11... | collective-permute-start | bytes 430088 | tf_op jit(solution)/shard_map/ppermute | solution.py:19
  18.4 2.3 %collective-permute-start.7 = (bf16[40,1792]{1,0:T(8,128)(2,1)S(1)}, bf16[40,1792]{1,0:T(8,128)(2,1)S(1)}, u32[]{:S(2)}, u32[]{:S(2)}) collective-permute-start(bf16[40,1792]{1,0:T(8,128)(2,1)S(1)} %collective-permute-done.3.refs_3_), channel_id=1, source_target_pairs={{0,1},{1,0},{2,3},{3,2},{4,5},{5,4},{6,7},{7,6},{8,9},{9,8},{10,11... | collective-permute-start | bytes 430088 | tf_op jit(solution)/shard_map/ppermute | solution.py:19
  20.7 1.0 %collective-permute-done.7.refs_7_ = bf16[40,1792]{1,0:T(8,128)(2,1)S(1)} collective-permute-done((bf16[40,1792]{1,0:T(8,128)(2,1)S(1)}, bf16[40,1792]{1,0:T(8,128)(2,1)S(1)}, u32[]{:S(2)}, u32[]{:S(2)}) %collective-permute-start.7) | collective-permute-done | bytes 143392 | tf_op jit(solution)/shard_map/ppermute | solution.py:19
  21.7 18.4 %experts.1 = (f32[80,3584]{1,0:T(8,128)S(1)}, bf16[80,3584]{1,0:T(8,128)(2,1)S(1)}) custom-call(bf16[40,1792]{1,0:T(8,128)(2,1)S(1)} %collective-permute-done.refs_0_, bf16[40,1792]{1,0:T(8,128)(2,1)S(1)} %collective-permute-done.1.refs_1_, bf16[40,1792]{1,0:T(8,128)(2,1)S(1)} %collective-permute-done.2.refs_2_, ...), custom_call_target="tpu_custom_call" | custom-call | tf_op jit(solution)/shard_map/experts/pallas_call | solution.py:250
  40.6 1.6 %collective-permute-done.8.got_ref = bf16[80,3584]{1,0:T(8,128)(2,1)S(1)} collective-permute-done((bf16[80,3584]{1,0:T(8,128)(2,1)S(1)}, bf16[80,3584]{1,0:T(8,128)(2,1)S(1)}, u32[]{:S(2)}, u32[]{:S(2)}) %collective-permute-start.8) | collective-permute-done | bytes 573472 | tf_op jit(solution)/shard_map/ppermute | solution.py:19
  42.5 0.7 %collective-permute-start.9 = (bf16[40,1792]{1,0:T(8,128)(2,1)S(1)}, bf16[40,1792]{1,0:T(8,128)(2,1)S(1)}, u32[]{:S(2)}, u32[]{:S(2)}) collective-permute-start(bf16[40,1792]{1,0:T(8,128)(2,1)S(1)} %get-tuple-element.25), channel_id=1, source_target_pairs={{0,0},{1,9},{2,2},{3,11},{4,4},{5,13},{6,6},{7,15},{8,8},{9,1},{10... | collective-permute-start | bytes 430088 | tf_op jit(solution)/shard_map/ppermute | solution.py:227
  43.2 0.7 %collective-permute-start.10 = (bf16[40,1792]{1,0:T(8,128)(2,1)S(1)}, bf16[40,1792]{1,0:T(8,128)(2,1)S(1)}, u32[]{:S(2)}, u32[]{:S(2)}) collective-permute-start(bf16[40,1792]{1,0:T(8,128)(2,1)S(1)} %get-tuple-element.26), channel_id=1, source_target_pairs={{0,2},{1,11},{2,0},{3,9},{4,6},{5,15},{6,4},{7,13},{8,10},{9,3},{1... | collective-permute-start | bytes 430088 | tf_op jit(solution)/shard_map/ppermute | solution.py:227
  44.0 2.9 %collective-permute-start.11 = (bf16[40,1792]{1,0:T(8,128)(2,1)S(1)}, bf16[40,1792]{1,0:T(8,128)(2,1)S(1)}, u32[]{:S(2)}, u32[]{:S(2)}) collective-permute-start(bf16[40,1792]{1,0:T(8,128)(2,1)S(1)} %get-tuple-element.27), channel_id=1, source_target_pairs={{0,4},{1,13},{2,6},{3,15},{4,0},{5,9},{6,2},{7,11},{8,12},{9,5},{1... | collective-permute-start | bytes 430088 | tf_op jit(solution)/shard_map/ppermute | solution.py:227
  47.4 1.0 %collective-permute-done.10.refs_1_ = bf16[40,1792]{1,0:T(8,128)(2,1)S(1)} collective-permute-done((bf16[40,1792]{1,0:T(8,128)(2,1)S(1)}, bf16[40,1792]{1,0:T(8,128)(2,1)S(1)}, u32[]{:S(2)}, u32[]{:S(2)}) %collective-permute-start.10) | collective-permute-done | bytes 143392 | tf_op jit(solution)/shard_map/ppermute | solution.py:227
  48.4 1.5 %collective-permute-done.11.refs_2_ = bf16[40,1792]{1,0:T(8,128)(2,1)S(1)} collective-permute-done((bf16[40,1792]{1,0:T(8,128)(2,1)S(1)}, bf16[40,1792]{1,0:T(8,128)(2,1)S(1)}, u32[]{:S(2)}, u32[]{:S(2)}) %collective-permute-start.11) | collective-permute-done | bytes 143392 | tf_op jit(solution)/shard_map/ppermute | solution.py:227
  49.9 3.2 %collective-permute-done.12.refs_3_ = bf16[40,1792]{1,0:T(8,128)(2,1)S(1)} collective-permute-done((bf16[40,1792]{1,0:T(8,128)(2,1)S(1)}, bf16[40,1792]{1,0:T(8,128)(2,1)S(1)}, u32[]{:S(2)}, u32[]{:S(2)}) %collective-permute-start.12) | collective-permute-done | bytes 143392 | tf_op jit(solution)/shard_map/ppermute | solution.py:227
  53.2 0.5 combine.1
  53.7 6.8 %collective-permute-start.13 = (bf16[64,1792]{1,0:T(8,128)(2,1)S(1)}, bf16[64,1792]{1,0:T(8,128)(2,1)S(1)}, u32[]{:S(2)}, u32[]{:S(2)}) collective-permute-start(bf16[64,1792]{1,0:T(8,128)(2,1)S(1)} %get-tuple-element.30), channel_id=1, source_target_pairs={{0,1},{1,0},{2,3},{3,2},{4,5},{5,4},{6,7},{7,6},{8,9},{9,8},{10,11... | collective-permute-start | bytes 688136 | tf_op jit(solution)/shard_map/ppermute | solution.py:19
  60.4 1.1 %collective-permute-done.13 = bf16[64,1792]{1,0:T(8,128)(2,1)S(1)} collective-permute-done((bf16[64,1792]{1,0:T(8,128)(2,1)S(1)}, bf16[64,1792]{1,0:T(8,128)(2,1)S(1)}, u32[]{:S(2)}, u32[]{:S(2)}) %collective-permute-start.13) | collective-permute-done | bytes 229408 | tf_op jit(solution)/shard_map/ppermute | solution.py:19
  61.6 0.7 %add_convert_fusion = bf16[64,1792]{1,0:T(8,128)(2,1)} fusion(f32[64,1792]{1,0:T(8,128)S(1)} %get-tuple-element.29, bf16[64,1792]{1,0:T(8,128)(2,1)S(1)} %collective-permute-done.13), kind=kLoop, calls=%fused_computation | loop fusion | flops 344064 | bytes 917504 | tf_op jit(solution)/shard_map/convert_element_type | solution.py:294
  (17 shorter events, 1.3 us)
Async XLA Ops:
  0.0 1.0 %copy-start = (bf16[64,3584]{1,0:T(8,128)(2,1)S(1)}, bf16[64,3584]{1,0:T(8,128)(2,1)}, u32[]{:S(2)}) copy-start(bf16[64,3584]{1,0:T(8,128)(2,1)} %tok_ref.1) | copy-start | bytes 1376260
  1.0 0.7 %copy-start.1 = (s32[64,2]{0,1:T(2,128)S(1)}, s32[64,2]{0,1:T(2,128)}, u32[]{:S(2)}) copy-start(s32[64,2]{0,1:T(2,128)} %param.8) | copy-start | bytes 1540
  1.7 0.7 %copy-start.3 = (s32[32]{0:T(128)S(1)}, s32[32]{0:T(128)}, u32[]{:S(2)}) copy-start(s32[32]{0:T(128)} %param.10) | copy-start | bytes 388
  3.0 5.3 %collective-permute-start = (bf16[40,1792]{1,0:T(8,128)(2,1)S(1)}, bf16[40,1792]{1,0:T(8,128)(2,1)S(1)}, u32[]{:S(2)}, u32[]{:S(2)}) collective-permute-start(bf16[40,1792]{1,0:T(8,128)(2,1)S(1)} %get-tuple-element.19), channel_id=1, source_target_pairs={{0,0},{1,9},{2,2},{3,11},{4,4},{5,13},{6,6},{7,15},{8,8},{9,1},{10... | collective-permute-start | bytes 430088 | tf_op jit(solution)/shard_map/ppermute | solution.py:227
  3.7 9.3 %collective-permute-start.1 = (bf16[40,1792]{1,0:T(8,128)(2,1)S(1)}, bf16[40,1792]{1,0:T(8,128)(2,1)S(1)}, u32[]{:S(2)}, u32[]{:S(2)}) collective-permute-start(bf16[40,1792]{1,0:T(8,128)(2,1)S(1)} %get-tuple-element.20), channel_id=1, source_target_pairs={{0,2},{1,11},{2,0},{3,9},{4,6},{5,15},{6,4},{7,13},{8,10},{9,3},{1... | collective-permute-start | bytes 430088 | tf_op jit(solution)/shard_map/ppermute | solution.py:227
  6.7 9.5 %collective-permute-start.2 = (bf16[40,1792]{1,0:T(8,128)(2,1)S(1)}, bf16[40,1792]{1,0:T(8,128)(2,1)S(1)}, u32[]{:S(2)}, u32[]{:S(2)}) collective-permute-start(bf16[40,1792]{1,0:T(8,128)(2,1)S(1)} %get-tuple-element.21), channel_id=1, source_target_pairs={{0,4},{1,13},{2,6},{3,15},{4,0},{5,9},{6,2},{7,11},{8,12},{9,5},{1... | collective-permute-start | bytes 430088 | tf_op jit(solution)/shard_map/ppermute | solution.py:227
  8.3 44.9 %copy-start.2 = (f32[64,2]{0,1:T(2,128)S(1)}, f32[64,2]{0,1:T(2,128)}, u32[]{:S(2)}) copy-start(f32[64,2]{0,1:T(2,128)} %param.9) | copy-start | bytes 1540
  8.3 10.1 %collective-permute-start.3 = (bf16[40,1792]{1,0:T(8,128)(2,1)S(1)}, bf16[40,1792]{1,0:T(8,128)(2,1)S(1)}, u32[]{:S(2)}, u32[]{:S(2)}) collective-permute-start(bf16[40,1792]{1,0:T(8,128)(2,1)S(1)} %get-tuple-element.22), channel_id=1, source_target_pairs={{0,6},{1,15},{2,4},{3,13},{4,2},{5,11},{6,0},{7,9},{8,14},{9,7},{1... | collective-permute-start | bytes 430088 | tf_op jit(solution)/shard_map/ppermute | solution.py:227
  8.3 12.4 %collective-permute-start.4 = (bf16[40,1792]{1,0:T(8,128)(2,1)S(1)}, bf16[40,1792]{1,0:T(8,128)(2,1)S(1)}, u32[]{:S(2)}, u32[]{:S(2)}) collective-permute-start(bf16[40,1792]{1,0:T(8,128)(2,1)S(1)} %collective-permute-done.refs_0_), channel_id=1, source_target_pairs={{0,1},{1,0},{2,3},{3,2},{4,5},{5,4},{6,7},{7,6},{8,9},{9,8},{10,11... | collective-permute-start | bytes 430088 | tf_op jit(solution)/shard_map/ppermute | solution.py:19
  13.0 7.7 %collective-permute-start.5 = (bf16[40,1792]{1,0:T(8,128)(2,1)S(1)}, bf16[40,1792]{1,0:T(8,128)(2,1)S(1)}, u32[]{:S(2)}, u32[]{:S(2)}) collective-permute-start(bf16[40,1792]{1,0:T(8,128)(2,1)S(1)} %collective-permute-done.1.refs_1_), channel_id=1, source_target_pairs={{0,1},{1,0},{2,3},{3,2},{4,5},{5,4},{6,7},{7,6},{8,9},{9,8},{10,11... | collective-permute-start | bytes 430088 | tf_op jit(solution)/shard_map/ppermute | solution.py:19
  16.2 4.5 %collective-permute-start.6 = (bf16[40,1792]{1,0:T(8,128)(2,1)S(1)}, bf16[40,1792]{1,0:T(8,128)(2,1)S(1)}, u32[]{:S(2)}, u32[]{:S(2)}) collective-permute-start(bf16[40,1792]{1,0:T(8,128)(2,1)S(1)} %collective-permute-done.2.refs_2_), channel_id=1, source_target_pairs={{0,1},{1,0},{2,3},{3,2},{4,5},{5,4},{6,7},{7,6},{8,9},{9,8},{10,11... | collective-permute-start | bytes 430088 | tf_op jit(solution)/shard_map/ppermute | solution.py:19
  18.4 3.3 %collective-permute-start.7 = (bf16[40,1792]{1,0:T(8,128)(2,1)S(1)}, bf16[40,1792]{1,0:T(8,128)(2,1)S(1)}, u32[]{:S(2)}, u32[]{:S(2)}) collective-permute-start(bf16[40,1792]{1,0:T(8,128)(2,1)S(1)} %collective-permute-done.3.refs_3_), channel_id=1, source_target_pairs={{0,1},{1,0},{2,3},{3,2},{4,5},{5,4},{6,7},{7,6},{8,9},{9,8},{10,11... | collective-permute-start | bytes 430088 | tf_op jit(solution)/shard_map/ppermute | solution.py:19
  40.2 2.0 %collective-permute-start.8 = (bf16[80,3584]{1,0:T(8,128)(2,1)S(1)}, bf16[80,3584]{1,0:T(8,128)(2,1)S(1)}, u32[]{:S(2)}, u32[]{:S(2)}) collective-permute-start(bf16[80,3584]{1,0:T(8,128)(2,1)S(1)} %get-tuple-element.24), channel_id=1, source_target_pairs={{0,1},{1,0},{2,3},{3,2},{4,5},{5,4},{6,7},{7,6},{8,9},{9,8},{10,11... | collective-permute-start | bytes 1720328 | tf_op jit(solution)/shard_map/ppermute | solution.py:19
  42.5 4.8 %collective-permute-start.9 = (bf16[40,1792]{1,0:T(8,128)(2,1)S(1)}, bf16[40,1792]{1,0:T(8,128)(2,1)S(1)}, u32[]{:S(2)}, u32[]{:S(2)}) collective-permute-start(bf16[40,1792]{1,0:T(8,128)(2,1)S(1)} %get-tuple-element.25), channel_id=1, source_target_pairs={{0,0},{1,9},{2,2},{3,11},{4,4},{5,13},{6,6},{7,15},{8,8},{9,1},{10... | collective-permute-start | bytes 430088 | tf_op jit(solution)/shard_map/ppermute | solution.py:227
  43.2 5.2 %collective-permute-start.10 = (bf16[40,1792]{1,0:T(8,128)(2,1)S(1)}, bf16[40,1792]{1,0:T(8,128)(2,1)S(1)}, u32[]{:S(2)}, u32[]{:S(2)}) collective-permute-start(bf16[40,1792]{1,0:T(8,128)(2,1)S(1)} %get-tuple-element.26), channel_id=1, source_target_pairs={{0,2},{1,11},{2,0},{3,9},{4,6},{5,15},{6,4},{7,13},{8,10},{9,3},{1... | collective-permute-start | bytes 430088 | tf_op jit(solution)/shard_map/ppermute | solution.py:227
  44.0 6.0 %collective-permute-start.11 = (bf16[40,1792]{1,0:T(8,128)(2,1)S(1)}, bf16[40,1792]{1,0:T(8,128)(2,1)S(1)}, u32[]{:S(2)}, u32[]{:S(2)}) collective-permute-start(bf16[40,1792]{1,0:T(8,128)(2,1)S(1)} %get-tuple-element.27), channel_id=1, source_target_pairs={{0,4},{1,13},{2,6},{3,15},{4,0},{5,9},{6,2},{7,11},{8,12},{9,5},{1... | collective-permute-start | bytes 430088 | tf_op jit(solution)/shard_map/ppermute | solution.py:227
  46.8 6.3 %collective-permute-start.12 = (bf16[40,1792]{1,0:T(8,128)(2,1)S(1)}, bf16[40,1792]{1,0:T(8,128)(2,1)S(1)}, u32[]{:S(2)}, u32[]{:S(2)}) collective-permute-start(bf16[40,1792]{1,0:T(8,128)(2,1)S(1)} %get-tuple-element.28), channel_id=1, source_target_pairs={{0,6},{1,15},{2,4},{3,13},{4,2},{5,11},{6,0},{7,9},{8,14},{9,7},{1... | collective-permute-start | bytes 430088 | tf_op jit(solution)/shard_map/ppermute | solution.py:227
  53.7 7.9 %collective-permute-start.13 = (bf16[64,1792]{1,0:T(8,128)(2,1)S(1)}, bf16[64,1792]{1,0:T(8,128)(2,1)S(1)}, u32[]{:S(2)}, u32[]{:S(2)}) collective-permute-start(bf16[64,1792]{1,0:T(8,128)(2,1)S(1)} %get-tuple-element.30), channel_id=1, source_target_pairs={{0,1},{1,0},{2,3},{3,2},{4,5},{5,4},{6,7},{7,6},{8,9},{9,8},{10,11... | collective-permute-start | bytes 688136 | tf_op jit(solution)/shard_map/ppermute | solution.py:19

commit v2 on v1

--- a/solution.py
+++ b/solution.py
@@ -11,7 +11,10 @@
 SLOTS = 32
 EXPERTS = 28
 CAP = 5
-STEP_BLOCKS = 2
+UNROLL = 8
+COLUMNS = 512
+LIMIT = 14
+RING = 4
 MIB = 1 << 20
 
 
@@ -98,7 +101,14 @@
     return lax.dot_general(left, right, dims, preferred_element_type=jnp.float32)
 
 
-def pick_kernel(slots_dev, key_ref, ids_ref, plan_ref, tok_ref, pick_ref, *send_refs):
+def pick_kernel(slots_dev, key_ref, ids_hbm, plan_hbm, tok_hbm, pick_ref, *refs):
+    send_refs, (ids_ref, plan_ref, tok_ref, sems) = refs[:-4], refs[-4:]
+    pairs = ((tok_hbm, tok_ref), (ids_hbm, ids_ref), (plan_hbm, plan_ref))
+    loads = [pltpu.make_async_copy(a, b, sems.at[i]) for i, (a, b) in enumerate(pairs)]
+    for load in loads:
+        load.start()
+    loads[1].wait()
+    loads[2].wait()
     rounds = len(send_refs)
     rows = slots_dev * CAP
     packed = 2 * rows * rounds
@@ -129,48 +139,72 @@
     in_row = dot(onehot(either), before) == rank.astype(jnp.float32)
     for k, mask in enumerate(named):
         pick_ref[k, :, :] = onehot(mask & in_row)
+    loads[0].wait()
     stacked = jnp.concatenate([tok_ref[:, :half], tok_ref[:, half:]], axis=0)
     sent = dot(onehot(either & in_row), stacked).astype(jnp.bfloat16)
     for p, send_ref in enumerate(send_refs):
         send_ref[...] = sent[2 * rows * p : 2 * rows * (p + 1), :]
 
 
+def fetch_kernel(*refs):
+    count = (len(refs) - 2) // 2
+    sems = refs[-1]
+    pieces = sems.shape[1]
+    loads = []
+    for a in range(count):
+        source, target = refs[1 + a], refs[1 + count + a]
+        size = source.shape[0] // pieces
+        for i in range(pieces):
+            piece = pl.ds(i * size, size)
+            loads.append(pltpu.make_async_copy(source.at[piece], target.at[piece], sems.at[a, i]))
+    for load in loads:
+        load.start()
+    for load in loads:
+        load.wait()
+
+
 def expert_kernel(slots_dev, bufs, *refs):
     buf_refs = refs[:bufs]
-    gate_ref, up_ref, down_ref, mine_ref, other_ref, x_ref, acc_ref = refs[bufs:]
+    gate_ref, up_ref, down_hbm, mine_ref, other_ref, x_ref, hidden_ref, down_ref, sems = refs[bufs:]
+    ring, blocks, unit, chunk = down_ref.shape
+    chunks = down_hbm.shape[2] // chunk
+    loads = []
+    for i in range(chunks):
+        source = down_hbm.at[:, :, pl.ds(i * chunk, chunk)]
+        loads.append(pltpu.make_async_copy(source, down_ref.at[i % ring], sems.at[i]))
+    for load in loads[:ring]:
+        load.start()
     rows = slots_dev * CAP
     total = bufs * rows
     half = buf_refs[0].shape[1]
-    step = pl.program_id(0)
-
-    @pl.when(step == 0)
-    def _():
-        got = jnp.concatenate([ref[...] for ref in buf_refs], axis=0)
-        place = iota((total, 2 * total), 0)
-        place = place + rows * quotient(place, rows)
-        lane = iota((total, 2 * total), 1)
-        x_ref[:, :half] = dot(onehot(lane == place), got).astype(jnp.bfloat16)
-        x_ref[:, half:] = dot(onehot(lane == place + rows), got).astype(jnp.bfloat16)
-        acc_ref[...] = jnp.zeros_like(acc_ref)
-
-    x = x_ref[...]
+
+    got = jnp.concatenate([ref[...] for ref in buf_refs], axis=0)
+    place = iota((total, 2 * total), 0)
+    place = place + rows * quotient(place, rows)
+    lane = iota((total, 2 * total), 1)
+    x_ref[:, :half] = dot(onehot(lane == place), got).astype(jnp.bfloat16)
+    x_ref[:, half:] = dot(onehot(lane == place + rows), got).astype(jnp.bfloat16)
+
     index = iota((total, 1), 0)
     row_slot = quotient(index, CAP) - quotient(index, rows) * slots_dev
-    hidden = []
-    for b in range(STEP_BLOCKS):
-        both = dot(x, jnp.concatenate([gate_ref[b], up_ref[b]], axis=1))
-        unit = gate_ref.shape[2]
+
+    def block(b, carry):
+        both = dot(x_ref[...], jnp.concatenate([gate_ref[b], up_ref[b]], axis=1))
         gate, upper = both[:, :unit], both[:, unit:]
         value = gate / (1.0 + jnp.exp(-gate)) * upper
-        mine = row_slot == (step * STEP_BLOCKS + b) // HB
-        hidden.append(jnp.where(mine, value, 0.0).astype(jnp.bfloat16))
-    down = jnp.concatenate([down_ref[b] for b in range(STEP_BLOCKS)], axis=0)
-    acc_ref[...] += dot(jnp.concatenate(hidden, axis=1), down)
-
-    @pl.when(step == pl.num_programs(0) - 1)
-    def _():
-        mine_ref[...] = acc_ref[: total // 2, :]
-        other_ref[...] = acc_ref[total // 2 :, :].astype(jnp.bfloat16)
+        hidden_ref[b] = jnp.where(row_slot == b // HB, value, 0.0).astype(jnp.bfloat16)
+        return carry
+
+    lax.fori_loop(0, blocks, block, 0, unroll=UNROLL)
+    hidden = jnp.concatenate([hidden_ref[b] for b in range(blocks)], axis=1)
+    for i in range(chunks):
+        cols = slice(i * chunk, (i + 1) * chunk)
+        loads[i].wait()
+        part = dot(hidden, down_ref[i % ring].reshape(blocks * unit, chunk))
+        mine_ref[:, cols] = part[: total // 2, :]
+        other_ref[:, cols] = part[total // 2 :, :].astype(jnp.bfloat16)
+        if i + ring < chunks:
+            loads[i + ring].start()
 
 
 def sum_kernel(rows, mine_ref, got_ref, *send_refs):
@@ -201,8 +235,14 @@
     give_ref[...] = sum_ref[pl.ds(pl.multiple_of((1 - core) * tok_rows, 8), tok_rows), :].astype(jnp.bfloat16)
 
 
+ANY = pl.BlockSpec(memory_space=pl.ANY)
+HBM = pl.BlockSpec(memory_space=pltpu.HBM)
 VMEM = pl.BlockSpec(memory_space=pltpu.VMEM)
 SMEM = pl.BlockSpec(memory_space=pltpu.SMEM)
+
+
+def from_hbm(array):
+    return pltpu.with_memory_space_constraint(array, pltpu.HBM)
 
 
 def params(mib):
@@ -235,39 +275,52 @@
     pick, *sent = pl.pallas_call(
         functools.partial(pick_kernel, slots_dev),
         out_shape=[jax.ShapeDtypeStruct((picks, 2 * rows * rounds, 2 * tok_rows), jnp.bfloat16)] + [packed] * rounds,
-        in_specs=[SMEM, VMEM, VMEM, VMEM],
+        in_specs=[SMEM, HBM, HBM, HBM],
         out_specs=[VMEM] * (1 + rounds),
+        scratch_shapes=[
+            pltpu.VMEM((picks, tok_rows), jnp.int32),
+            pltpu.VMEM((1, slot_plan.shape[0]), jnp.int32),
+            pltpu.VMEM((tok_rows, width), jnp.bfloat16),
+            pltpu.SemaphoreType.DMA((3,)),
+        ],
         compiler_params=params(16),
         name="pick_rows",
-    )(key, expert_ids.T, slot_plan.reshape(1, -1), tokens)
-
-    got = travel(sent)
+    )(key, *[from_hbm(a) for a in (expert_ids.T, slot_plan.reshape(1, -1), tokens)])
+
+    weights = [w_gate, w_up]
+    held = pl.pallas_call(
+            fetch_kernel,
+            out_shape=[pltpu.VMEM(w.shape, w.dtype) for w in weights[:2]],
+            in_specs=[ANY] + [HBM] * 2,
+            out_specs=[ANY] * 2,
+            scratch_shapes=[pltpu.SemaphoreType.DMA((2, 4))],
+            compiler_params=params(1),
+            cost_estimate=pl.CostEstimate(flops=0, bytes_accessed=2 * 2 * w_gate.size, transcendentals=0),
+            name="fetch",
+        )(sent[-1], *[from_hbm(w) for w in weights])
+
+    got, held = lax.optimization_barrier((travel(sent), held))
     got = got + [swapped(array, "tensor", 0) for array in got]
 
     total = chips * rows
     blocks, _, unit = w_gate.shape
-    whole = lambda shape: pl.BlockSpec(shape, lambda i: (0, 0))
     mine, other = pl.pallas_call(
         functools.partial(expert_kernel, slots_dev, chips),
-        grid=(blocks // STEP_BLOCKS,),
         out_shape=[
             jax.ShapeDtypeStruct((total // 2, width), jnp.float32),
             jax.ShapeDtypeStruct((total // 2, width), jnp.bfloat16),
         ],
-        in_specs=[whole((2 * rows, half))] * chips
-        + [
-            pl.BlockSpec((STEP_BLOCKS, width, unit), lambda i: (i, 0, 0)),
-            pl.BlockSpec((STEP_BLOCKS, width, unit), lambda i: (i, 0, 0)),
-            pl.BlockSpec((STEP_BLOCKS, unit, width), lambda i: (i, 0, 0)),
-        ],
-        out_specs=[whole((total // 2, width))] * 2,
+        in_specs=[VMEM] * (chips + 2) + [HBM],
+        out_specs=[VMEM] * 2,
         scratch_shapes=[
             pltpu.VMEM((total, width), jnp.bfloat16),
-            pltpu.VMEM((total, width), jnp.float32),
+            pltpu.VMEM((blocks, total, unit), jnp.bfloat16),
+            pltpu.VMEM((RING, blocks, unit, COLUMNS), jnp.bfloat16),
+            pltpu.SemaphoreType.DMA((width // COLUMNS,)),
         ],
-        compiler_params=params(40),
+        compiler_params=params(LIMIT),
         name="experts",
-    )(*got, w_gate, w_up, w_down)
+    )(*got, *held, from_hbm(w_down))
 
     back = pl.pallas_call(
         functools.partial(sum_kernel, rows),

time: 63.1 us -> 55.2 us (0.87)
  starting transfers between devices: 29.7 us -> 20 us
  local copies, waits for them, and re-layouts: 2.35 us -> 0.01 us
  waiting for transfers between devices: 9.55 us -> 11.5 us
  Pallas kernels: 19.9 us -> 21.8 us
    ppermute x6, starting transfers between devices: 19.6 us -> 10.6 us  [swapped(): lax.ppermute(shard, axis, [(i, i ^ 1 << stride) for i in range(lax.axis_s...]
    unnamed x8 -> x2, local copies, waits for them, and re-layouts: 2.35 us -> 0.01 us
    ppermute x8, waiting for transfers between devices: 5.81 us -> 7.31 us  [travel(): lax.ppermute(array, ('expert', 'tensor'), [(2 * i + c, 2 * (i ^ p + round...]
    pallas_call x1 -> x2, Pallas kernels: 18.4 us -> 19.4 us  [the longest x1 9.95 us: shards_paired(): pl.pallas_call(functools.partial(expert_kernel, slots_dev, chips), out_sh...]
    pallas_call x1, Pallas kernels: 0.63 us -> 1.51 us  [shards_paired(): pl.pallas_call(functools.partial(pick_kernel, slots_dev), out_shape=[jax....]
  transfers between devices with their start and end apart: 14 -> 14, of which waited for: 6 -> 9; matrix products, arithmetic and copies ran while one was open for 0% -> 0% of each run, Pallas kernels for 0% -> 18%
where the time goes in v2:
time: 55.2 us; the launch traced here: 54.2 us
  Pallas kernels  21.8 us (39%)
  starting transfers between devices  20 us (36%)
  waiting for transfers between devices  11.5 us (21%)
  other arithmetic  0.74 us (1%)
    ppermute x6, starting transfers between devices, swapped(): lax.ppermute(shard, axis, [(i, i ^ 1 << stride) for i in range(lax.axis_s...  10.6 us
    pallas_call x1, Pallas kernels, shards_paired(): pl.pallas_call(functools.partial(expert_kernel, slots_dev, chips), out_sh...  9.95 us
    pallas_call x1, Pallas kernels, shards_paired(): pl.pallas_call(fetch_kernel, out_shape=[pltpu.VMEM(w.shape, w.dtype) for...  9.49 us
    ppermute x8, starting transfers between devices, travel(): lax.ppermute(array, ('expert', 'tensor'), [(2 * i + c, 2 * (i ^ p + round...  9.48 us
    ppermute x8, waiting for transfers between devices, travel(): lax.ppermute(array, ('expert', 'tensor'), [(2 * i + c, 2 * (i ^ p + round...  7.31 us
    ppermute x6, waiting for transfers between devices, swapped(): lax.ppermute(shard, axis, [(i, i ^ 1 << stride) for i in range(lax.axis_s...  4.18 us
    pallas_call x1, Pallas kernels, shards_paired(): pl.pallas_call(functools.partial(pick_kernel, slots_dev), out_shape=[jax....  1.51 us
  transfers between devices with their start and end apart: 14, of which 9 were waited for; matrix products, arithmetic and copies ran while one was open for 0% of the time, Pallas kernels for 18%

profile of v2, /device:TPU:0, one launch (start us, length us, event | category | flops | bytes accessed | tf_op | source)
XLA Modules:
  0.0 54.2 jit_solution(6149211703409723222)
XLA Ops:
  0.0 1.5 %pick_rows.1 = (bf16[2,160,128]{2,1,0:T(8,128)(2,1)S(1)}, bf16[40,1792]{1,0:T(8,128)(2,1)S(1)}, bf16[40,1792]{1,0:T(8,128)(2,1)S(1)}, bf16[40,1792]{1,0:T(8,128)(2,1)S(1)}, bf16[40,1792]{1,0:T(8,128)(2,1)S(1)}) custom-call(s32[1]{0:T(128)} %bitcast.1.key_ref, s32[2,64]{1,0:T(2,128)} %bitcast.6, s32[1,32]{1,0:T(1,128)} %bitcast.7, bf16[64,3584]{1,0:T(8,128)(2,1)} %tok_hbm.1), custom_call_target="tpu_custom_call" | custom-call | tf_op jit(solution)/shard_map/pick_rows/pallas_call | solution.py:275
  1.5 0.7 %collective-permute-start = (bf16[40,1792]{1,0:T(8,128)(2,1)S(1)}, bf16[40,1792]{1,0:T(8,128)(2,1)S(1)}, u32[]{:S(2)}, u32[]{:S(2)}) collective-permute-start(bf16[40,1792]{1,0:T(8,128)(2,1)S(1)} %get-tuple-element.27), channel_id=1, source_target_pairs={{0,0},{1,9},{2,2},{3,11},{4,4},{5,13},{6,6},{7,15},{8,8},{9,1},{10... | collective-permute-start | bytes 430088 | tf_op jit(solution)/shard_map/ppermute | solution.py:267
  2.2 3.0 %collective-permute-start.1 = (bf16[40,1792]{1,0:T(8,128)(2,1)S(1)}, bf16[40,1792]{1,0:T(8,128)(2,1)S(1)}, u32[]{:S(2)}, u32[]{:S(2)}) collective-permute-start(bf16[40,1792]{1,0:T(8,128)(2,1)S(1)} %get-tuple-element.28), channel_id=1, source_target_pairs={{0,2},{1,11},{2,0},{3,9},{4,6},{5,15},{6,4},{7,13},{8,10},{9,3},{1... | collective-permute-start | bytes 430088 | tf_op jit(solution)/shard_map/ppermute | solution.py:267
  5.2 1.6 %collective-permute-start.2 = (bf16[40,1792]{1,0:T(8,128)(2,1)S(1)}, bf16[40,1792]{1,0:T(8,128)(2,1)S(1)}, u32[]{:S(2)}, u32[]{:S(2)}) collective-permute-start(bf16[40,1792]{1,0:T(8,128)(2,1)S(1)} %get-tuple-element.29), channel_id=1, source_target_pairs={{0,4},{1,13},{2,6},{3,15},{4,0},{5,9},{6,2},{7,11},{8,12},{9,5},{1... | collective-permute-start | bytes 430088 | tf_op jit(solution)/shard_map/ppermute | solution.py:267
  6.8 9.5 %fetch.1 = (bf16[16,3584,128]{2,1,0:T(8,128)(2,1)S(1)}, bf16[16,3584,128]{2,1,0:T(8,128)(2,1)S(1)}) custom-call(bf16[40,1792]{1,0:T(8,128)(2,1)S(1)} %get-tuple-element.30.refs_0_, bf16[16,3584,128]{2,1,0:T(8,128)(2,1)} %refs_1_.1, bf16[16,3584,128]{2,1,0:T(8,128)(2,1)} %refs_2_.1), custom_call_target="tpu_custom_call" | custom-call | bytes 29360128 | tf_op jit(solution)/shard_map/fetch/pallas_call | solution.py:291
  16.3 4.7 %collective-permute-start.4 = (bf16[40,1792]{1,0:T(8,128)(2,1)S(1)}, bf16[40,1792]{1,0:T(8,128)(2,1)S(1)}, u32[]{:S(2)}, u32[]{:S(2)}) collective-permute-start(bf16[40,1792]{1,0:T(8,128)(2,1)S(1)} %collective-permute-done.refs_0_), channel_id=1, source_target_pairs={{0,1},{1,0},{2,3},{3,2},{4,5},{5,4},{6,7},{7,6},{8,9},{9,8},{10,11... | collective-permute-start | bytes 430088 | tf_op jit(solution)/shard_map/ppermute | solution.py:22
  21.1 0.4 collective-permute-start.6
  21.6 0.4 collective-permute-done.4.refs_4_
  22.0 0.4 collective-permute-done.5.refs_5_
  22.6 0.3 collective-permute-done.7.refs_7_
  22.9 9.9 %experts.1 = (f32[80,3584]{1,0:T(8,128)S(1)}, bf16[80,3584]{1,0:T(8,128)(2,1)S(1)}) custom-call(bf16[40,1792]{1,0:T(8,128)(2,1)S(1)} %collective-permute-done.refs_0_, bf16[40,1792]{1,0:T(8,128)(2,1)S(1)} %collective-permute-done.1.refs_1_, bf16[40,1792]{1,0:T(8,128)(2,1)S(1)} %collective-permute-done.2.refs_2_, ...), custom_call_target="tpu_custom_call" | custom-call | tf_op jit(solution)/shard_map/experts/pallas_call | solution.py:307
  33.1 1.8 %collective-permute-done.8.got_ref = bf16[80,3584]{1,0:T(8,128)(2,1)S(1)} collective-permute-done((bf16[80,3584]{1,0:T(8,128)(2,1)S(1)}, bf16[80,3584]{1,0:T(8,128)(2,1)S(1)}, u32[]{:S(2)}, u32[]{:S(2)}) %collective-permute-start.8) | collective-permute-done | bytes 573472 | tf_op jit(solution)/shard_map/ppermute | solution.py:22
  34.9 0.3 sum_cores.1
  35.2 0.7 %collective-permute-start.9 = (bf16[40,1792]{1,0:T(8,128)(2,1)S(1)}, bf16[40,1792]{1,0:T(8,128)(2,1)S(1)}, u32[]{:S(2)}, u32[]{:S(2)}) collective-permute-start(bf16[40,1792]{1,0:T(8,128)(2,1)S(1)} %get-tuple-element.41), channel_id=1, source_target_pairs={{0,0},{1,9},{2,2},{3,11},{4,4},{5,13},{6,6},{7,15},{8,8},{9,1},{10... | collective-permute-start | bytes 430088 | tf_op jit(solution)/shard_map/ppermute | solution.py:267
  35.9 1.5 %collective-permute-start.10 = (bf16[40,1792]{1,0:T(8,128)(2,1)S(1)}, bf16[40,1792]{1,0:T(8,128)(2,1)S(1)}, u32[]{:S(2)}, u32[]{:S(2)}) collective-permute-start(bf16[40,1792]{1,0:T(8,128)(2,1)S(1)} %get-tuple-element.42), channel_id=1, source_target_pairs={{0,2},{1,11},{2,0},{3,9},{4,6},{5,15},{6,4},{7,13},{8,10},{9,3},{1... | collective-permute-start | bytes 430088 | tf_op jit(solution)/shard_map/ppermute | solution.py:267
  37.4 0.3 collective-permute-start.11
  37.7 1.7 %collective-permute-start.12 = (bf16[40,1792]{1,0:T(8,128)(2,1)S(1)}, bf16[40,1792]{1,0:T(8,128)(2,1)S(1)}, u32[]{:S(2)}, u32[]{:S(2)}) collective-permute-start(bf16[40,1792]{1,0:T(8,128)(2,1)S(1)} %get-tuple-element.44), channel_id=1, source_target_pairs={{0,6},{1,15},{2,4},{3,13},{4,2},{5,11},{6,0},{7,9},{8,14},{9,7},{1... | collective-permute-start | bytes 430088 | tf_op jit(solution)/shard_map/ppermute | solution.py:267
  39.5 1.6 %collective-permute-done.10.refs_1_ = bf16[40,1792]{1,0:T(8,128)(2,1)S(1)} collective-permute-done((bf16[40,1792]{1,0:T(8,128)(2,1)S(1)}, bf16[40,1792]{1,0:T(8,128)(2,1)S(1)}, u32[]{:S(2)}, u32[]{:S(2)}) %collective-permute-start.10) | collective-permute-done | bytes 143392 | tf_op jit(solution)/shard_map/ppermute | solution.py:267
  41.1 2.9 %collective-permute-done.11.refs_2_ = bf16[40,1792]{1,0:T(8,128)(2,1)S(1)} collective-permute-done((bf16[40,1792]{1,0:T(8,128)(2,1)S(1)}, bf16[40,1792]{1,0:T(8,128)(2,1)S(1)}, u32[]{:S(2)}, u32[]{:S(2)}) %collective-permute-start.11) | collective-permute-done | bytes 143392 | tf_op jit(solution)/shard_map/ppermute | solution.py:267
  44.0 2.8 %collective-permute-done.12.refs_3_ = bf16[40,1792]{1,0:T(8,128)(2,1)S(1)} collective-permute-done((bf16[40,1792]{1,0:T(8,128)(2,1)S(1)}, bf16[40,1792]{1,0:T(8,128)(2,1)S(1)}, u32[]{:S(2)}, u32[]{:S(2)}) %collective-permute-start.12) | collective-permute-done | bytes 143392 | tf_op jit(solution)/shard_map/ppermute | solution.py:267
  46.8 0.5 combine.1
  47.3 5.0 %collective-permute-start.13 = (bf16[64,1792]{1,0:T(8,128)(2,1)S(1)}, bf16[64,1792]{1,0:T(8,128)(2,1)S(1)}, u32[]{:S(2)}, u32[]{:S(2)}) collective-permute-start(bf16[64,1792]{1,0:T(8,128)(2,1)S(1)} %get-tuple-element.46), channel_id=1, source_target_pairs={{0,1},{1,0},{2,3},{3,2},{4,5},{5,4},{6,7},{7,6},{8,9},{9,8},{10,11... | collective-permute-start | bytes 688136 | tf_op jit(solution)/shard_map/ppermute | solution.py:22
  52.3 1.1 %collective-permute-done.13 = bf16[64,1792]{1,0:T(8,128)(2,1)S(1)} collective-permute-done((bf16[64,1792]{1,0:T(8,128)(2,1)S(1)}, bf16[64,1792]{1,0:T(8,128)(2,1)S(1)}, u32[]{:S(2)}, u32[]{:S(2)}) %collective-permute-start.13) | collective-permute-done | bytes 229408 | tf_op jit(solution)/shard_map/ppermute | solution.py:22
  53.4 0.7 %add_convert_fusion = bf16[64,1792]{1,0:T(8,128)(2,1)} fusion(f32[64,1792]{1,0:T(8,128)S(1)} %get-tuple-element.45, bf16[64,1792]{1,0:T(8,128)(2,1)S(1)} %collective-permute-done.13), kind=kLoop, calls=%fused_computation | loop fusion | flops 344064 | bytes 917504 | tf_op jit(solution)/shard_map/convert_element_type | solution.py:347
  (12 shorter events, 0.7 us)
Async XLA Ops:
  1.5 14.8 %collective-permute-start = (bf16[40,1792]{1,0:T(8,128)(2,1)S(1)}, bf16[40,1792]{1,0:T(8,128)(2,1)S(1)}, u32[]{:S(2)}, u32[]{:S(2)}) collective-permute-start(bf16[40,1792]{1,0:T(8,128)(2,1)S(1)} %get-tuple-element.27), channel_id=1, source_target_pairs={{0,0},{1,9},{2,2},{3,11},{4,4},{5,13},{6,6},{7,15},{8,8},{9,1},{10... | collective-permute-start | bytes 430088 | tf_op jit(solution)/shard_map/ppermute | solution.py:267
  2.2 14.1 %collective-permute-start.1 = (bf16[40,1792]{1,0:T(8,128)(2,1)S(1)}, bf16[40,1792]{1,0:T(8,128)(2,1)S(1)}, u32[]{:S(2)}, u32[]{:S(2)}) collective-permute-start(bf16[40,1792]{1,0:T(8,128)(2,1)S(1)} %get-tuple-element.28), channel_id=1, source_target_pairs={{0,2},{1,11},{2,0},{3,9},{4,6},{5,15},{6,4},{7,13},{8,10},{9,3},{1... | collective-permute-start | bytes 430088 | tf_op jit(solution)/shard_map/ppermute | solution.py:267
  5.2 11.1 %collective-permute-start.2 = (bf16[40,1792]{1,0:T(8,128)(2,1)S(1)}, bf16[40,1792]{1,0:T(8,128)(2,1)S(1)}, u32[]{:S(2)}, u32[]{:S(2)}) collective-permute-start(bf16[40,1792]{1,0:T(8,128)(2,1)S(1)} %get-tuple-element.29), channel_id=1, source_target_pairs={{0,4},{1,13},{2,6},{3,15},{4,0},{5,9},{6,2},{7,11},{8,12},{9,5},{1... | collective-permute-start | bytes 430088 | tf_op jit(solution)/shard_map/ppermute | solution.py:267
  6.8 9.5 %collective-permute-start.3 = (bf16[40,1792]{1,0:T(8,128)(2,1)S(1)}, bf16[40,1792]{1,0:T(8,128)(2,1)S(1)}, u32[]{:S(2)}, u32[]{:S(2)}) collective-permute-start(bf16[40,1792]{1,0:T(8,128)(2,1)S(1)} %get-tuple-element.30.refs_0_), channel_id=1, source_target_pairs={{0,6},{1,15},{2,4},{3,13},{4,2},{5,11},{6,0},{7,9},{8,14},{9,7},{1... | collective-permute-start | bytes 430088 | tf_op jit(solution)/shard_map/ppermute | solution.py:267
  16.3 30.5 %copy-start = (f32[64,2]{0,1:T(2,128)S(1)}, f32[64,2]{0,1:T(2,128)}, u32[]{:S(2)}) copy-start(f32[64,2]{0,1:T(2,128)} %param.9) | copy-start | bytes 1540
  16.3 5.7 %collective-permute-start.4 = (bf16[40,1792]{1,0:T(8,128)(2,1)S(1)}, bf16[40,1792]{1,0:T(8,128)(2,1)S(1)}, u32[]{:S(2)}, u32[]{:S(2)}) collective-permute-start(bf16[40,1792]{1,0:T(8,128)(2,1)S(1)} %collective-permute-done.refs_0_), channel_id=1, source_target_pairs={{0,1},{1,0},{2,3},{3,2},{4,5},{5,4},{6,7},{7,6},{8,9},{9,8},{10,11... | collective-permute-start | bytes 430088 | tf_op jit(solution)/shard_map/ppermute | solution.py:22
  21.0 1.4 %collective-permute-start.5 = (bf16[40,1792]{1,0:T(8,128)(2,1)S(1)}, bf16[40,1792]{1,0:T(8,128)(2,1)S(1)}, u32[]{:S(2)}, u32[]{:S(2)}) collective-permute-start(bf16[40,1792]{1,0:T(8,128)(2,1)S(1)} %collective-permute-done.1.refs_1_), channel_id=1, source_target_pairs={{0,1},{1,0},{2,3},{3,2},{4,5},{5,4},{6,7},{7,6},{8,9},{9,8},{10,11... | collective-permute-start | bytes 430088 | tf_op jit(solution)/shard_map/ppermute | solution.py:22
  21.1 1.5 %collective-permute-start.6 = (bf16[40,1792]{1,0:T(8,128)(2,1)S(1)}, bf16[40,1792]{1,0:T(8,128)(2,1)S(1)}, u32[]{:S(2)}, u32[]{:S(2)}) collective-permute-start(bf16[40,1792]{1,0:T(8,128)(2,1)S(1)} %collective-permute-done.2.refs_2_), channel_id=1, source_target_pairs={{0,1},{1,0},{2,3},{3,2},{4,5},{5,4},{6,7},{7,6},{8,9},{9,8},{10,11... | collective-permute-start | bytes 430088 | tf_op jit(solution)/shard_map/ppermute | solution.py:22
  21.5 1.4 %collective-permute-start.7 = (bf16[40,1792]{1,0:T(8,128)(2,1)S(1)}, bf16[40,1792]{1,0:T(8,128)(2,1)S(1)}, u32[]{:S(2)}, u32[]{:S(2)}) collective-permute-start(bf16[40,1792]{1,0:T(8,128)(2,1)S(1)} %collective-permute-done.3.refs_3_), channel_id=1, source_target_pairs={{0,1},{1,0},{2,3},{3,2},{4,5},{5,4},{6,7},{7,6},{8,9},{9,8},{10,11... | collective-permute-start | bytes 430088 | tf_op jit(solution)/shard_map/ppermute | solution.py:22
  32.9 2.0 %collective-permute-start.8 = (bf16[80,3584]{1,0:T(8,128)(2,1)S(1)}, bf16[80,3584]{1,0:T(8,128)(2,1)S(1)}, u32[]{:S(2)}, u32[]{:S(2)}) collective-permute-start(bf16[80,3584]{1,0:T(8,128)(2,1)S(1)} %get-tuple-element.40), channel_id=1, source_target_pairs={{0,1},{1,0},{2,3},{3,2},{4,5},{5,4},{6,7},{7,6},{8,9},{9,8},{10,11... | collective-permute-start | bytes 1720328 | tf_op jit(solution)/shard_map/ppermute | solution.py:22
  35.2 4.2 %collective-permute-start.9 = (bf16[40,1792]{1,0:T(8,128)(2,1)S(1)}, bf16[40,1792]{1,0:T(8,128)(2,1)S(1)}, u32[]{:S(2)}, u32[]{:S(2)}) collective-permute-start(bf16[40,1792]{1,0:T(8,128)(2,1)S(1)} %get-tuple-element.41), channel_id=1, source_target_pairs={{0,0},{1,9},{2,2},{3,11},{4,4},{5,13},{6,6},{7,15},{8,8},{9,1},{10... | collective-permute-start | bytes 430088 | tf_op jit(solution)/shard_map/ppermute | solution.py:267
  35.9 5.2 %collective-permute-start.10 = (bf16[40,1792]{1,0:T(8,128)(2,1)S(1)}, bf16[40,1792]{1,0:T(8,128)(2,1)S(1)}, u32[]{:S(2)}, u32[]{:S(2)}) collective-permute-start(bf16[40,1792]{1,0:T(8,128)(2,1)S(1)} %get-tuple-element.42), channel_id=1, source_target_pairs={{0,2},{1,11},{2,0},{3,9},{4,6},{5,15},{6,4},{7,13},{8,10},{9,3},{1... | collective-permute-start | bytes 430088 | tf_op jit(solution)/shard_map/ppermute | solution.py:267
  37.4 6.5 %collective-permute-start.11 = (bf16[40,1792]{1,0:T(8,128)(2,1)S(1)}, bf16[40,1792]{1,0:T(8,128)(2,1)S(1)}, u32[]{:S(2)}, u32[]{:S(2)}) collective-permute-start(bf16[40,1792]{1,0:T(8,128)(2,1)S(1)} %get-tuple-element.43), channel_id=1, source_target_pairs={{0,4},{1,13},{2,6},{3,15},{4,0},{5,9},{6,2},{7,11},{8,12},{9,5},{1... | collective-permute-start | bytes 430088 | tf_op jit(solution)/shard_map/ppermute | solution.py:267
  37.7 9.0 %collective-permute-start.12 = (bf16[40,1792]{1,0:T(8,128)(2,1)S(1)}, bf16[40,1792]{1,0:T(8,128)(2,1)S(1)}, u32[]{:S(2)}, u32[]{:S(2)}) collective-permute-start(bf16[40,1792]{1,0:T(8,128)(2,1)S(1)} %get-tuple-element.44), channel_id=1, source_target_pairs={{0,6},{1,15},{2,4},{3,13},{4,2},{5,11},{6,0},{7,9},{8,14},{9,7},{1... | collective-permute-start | bytes 430088 | tf_op jit(solution)/shard_map/ppermute | solution.py:267
  47.3 6.1 %collective-permute-start.13 = (bf16[64,1792]{1,0:T(8,128)(2,1)S(1)}, bf16[64,1792]{1,0:T(8,128)(2,1)S(1)}, u32[]{:S(2)}, u32[]{:S(2)}) collective-permute-start(bf16[64,1792]{1,0:T(8,128)(2,1)S(1)} %get-tuple-element.46), channel_id=1, source_target_pairs={{0,1},{1,0},{2,3},{3,2},{4,5},{5,4},{6,7},{7,6},{8,9},{9,8},{10,11... | collective-permute-start | bytes 688136 | tf_op jit(solution)/shard_map/ppermute | solution.py:22

commit v3 on v2

--- a/solution.py
+++ b/solution.py
@@ -12,9 +12,9 @@
 EXPERTS = 28
 CAP = 5
 UNROLL = 8
-COLUMNS = 512
-LIMIT = 14
-RING = 4
+COLUMNS = 896
+LIMIT = 15
+RING = 3
 MIB = 1 << 20
 
 
@@ -101,6 +101,10 @@
     return lax.dot_general(left, right, dims, preferred_element_type=jnp.float32)
 
 
+def turns(rounds):
+    return sorted(range(rounds), key=lambda p: (p < 2, p if p > 1 else -p))
+
+
 def pick_kernel(slots_dev, key_ref, ids_hbm, plan_hbm, tok_hbm, pick_ref, *refs):
     send_refs, (ids_ref, plan_ref, tok_ref, sems) = refs[:-4], refs[-4:]
     pairs = ((tok_hbm, tok_ref), (ids_hbm, ids_ref), (plan_hbm, plan_ref))
@@ -124,7 +128,9 @@
     part = quotient(index, rows)
     entry = quotient(index, CAP)
     rank = index - entry * CAP
-    slot = (key_ref[0] ^ lax.shift_right_logical(part, 1)) * slots_dev + entry - part * slots_dev
+    turn = lax.shift_right_logical(part, 1)
+    distance = sum(jnp.where(turn == q, p, 0) for q, p in enumerate(turns(rounds)))
+    slot = (key_ref[0] ^ distance) * slots_dev + entry - part * slots_dev
     side = part & 1
     chosen = jnp.where(iota((packed, slots), 1) == slot, served, 0)
     expert = jnp.sum(chosen, axis=1, keepdims=True)
@@ -269,7 +275,7 @@
                 ("expert", "tensor"),
                 [(2 * i + c, 2 * (i ^ (p + rounds * c)) + c) for i in range(chips) for c in range(2)],
             )
-            for p, array in enumerate(arrays)
+            for p, array in zip(turns(rounds), arrays)
         ]
 
     pick, *sent = pl.pallas_call(

time: 55.2 us -> 53.3 us (0.966); the launches traced: 54.2 us -> 53.2 us
  starting transfers between devices: 20 us -> 18.7 us
  waiting for transfers between devices: 11.5 us -> 12.2 us
    ppermute x6, starting transfers between devices: 10.6 us -> 9.17 us  [swapped(): lax.ppermute(shard, axis, [(i, i ^ 1 << stride) for i in range(lax.axis_s...]
    ppermute x8, waiting for transfers between devices: 7.31 us -> 8.06 us  [travel(): lax.ppermute(array, ('expert', 'tensor'), [(2 * i + c, 2 * (i ^ p + round...]
where the time goes in v3:
time: 53.3 us; the launch traced here: 53.2 us
  Pallas kernels  21.4 us (40%)
  starting transfers between devices  18.7 us (35%)
  waiting for transfers between devices  12.2 us (23%)
  other arithmetic  0.74 us (1%)
    pallas_call x1, Pallas kernels, shards_paired(): pl.pallas_call(functools.partial(expert_kernel, slots_dev, chips), out_sh...  9.56 us
    ppermute x8, starting transfers between devices, travel(): lax.ppermute(array, ('expert', 'tensor'), [(2 * i + c, 2 * (i ^ p + round...  9.5 us
    pallas_call x1, Pallas kernels, shards_paired(): pl.pallas_call(fetch_kernel, out_shape=[pltpu.VMEM(w.shape, w.dtype) for...  9.5 us
    ppermute x6, starting transfers between devices, swapped(): lax.ppermute(shard, axis, [(i, i ^ 1 << stride) for i in range(lax.axis_s...  9.17 us
    ppermute x8, waiting for transfers between devices, travel(): lax.ppermute(array, ('expert', 'tensor'), [(2 * i + c, 2 * (i ^ p + round...  8.06 us
    ppermute x6, waiting for transfers between devices, swapped(): lax.ppermute(shard, axis, [(i, i ^ 1 << stride) for i in range(lax.axis_s...  4.18 us
    pallas_call x1, Pallas kernels, shards_paired(): pl.pallas_call(functools.partial(pick_kernel, slots_dev), out_shape=[jax....  1.52 us
  transfers between devices with their start and end apart: 14, of which 9 were waited for; matrix products, arithmetic and copies ran while one was open for 0% of the time, Pallas kernels for 18%

profile of v3, /device:TPU:0, one launch (start us, length us, event | category | flops | bytes accessed | tf_op | source)
XLA Modules:
  0.0 53.2 jit_solution(468466592929971328)
XLA Ops:
  0.0 1.5 %pick_rows.1 = (bf16[2,160,128]{2,1,0:T(8,128)(2,1)S(1)}, bf16[40,1792]{1,0:T(8,128)(2,1)S(1)}, bf16[40,1792]{1,0:T(8,128)(2,1)S(1)}, bf16[40,1792]{1,0:T(8,128)(2,1)S(1)}, bf16[40,1792]{1,0:T(8,128)(2,1)S(1)}) custom-call(s32[1]{0:T(128)} %bitcast.1.key_ref, s32[2,64]{1,0:T(2,128)} %bitcast.6, s32[1,32]{1,0:T(1,128)} %bitcast.7, bf16[64,3584]{1,0:T(8,128)(2,1)} %tok_hbm.1), custom_call_target="tpu_custom_call" | custom-call | tf_op jit(solution)/shard_map/pick_rows/pallas_call | solution.py:281
  1.5 3.1 %collective-permute-start = (bf16[40,1792]{1,0:T(8,128)(2,1)S(1)}, bf16[40,1792]{1,0:T(8,128)(2,1)S(1)}, u32[]{:S(2)}, u32[]{:S(2)}) collective-permute-start(bf16[40,1792]{1,0:T(8,128)(2,1)S(1)} %get-tuple-element.27), channel_id=1, source_target_pairs={{0,4},{1,13},{2,6},{3,15},{4,0},{5,9},{6,2},{7,11},{8,12},{9,5},{1... | collective-permute-start | bytes 430088 | tf_op jit(solution)/shard_map/ppermute | solution.py:273
  4.6 1.4 %collective-permute-start.1 = (bf16[40,1792]{1,0:T(8,128)(2,1)S(1)}, bf16[40,1792]{1,0:T(8,128)(2,1)S(1)}, u32[]{:S(2)}, u32[]{:S(2)}) collective-permute-start(bf16[40,1792]{1,0:T(8,128)(2,1)S(1)} %get-tuple-element.28), channel_id=1, source_target_pairs={{0,6},{1,15},{2,4},{3,13},{4,2},{5,11},{6,0},{7,9},{8,14},{9,7},{1... | collective-permute-start | bytes 430088 | tf_op jit(solution)/shard_map/ppermute | solution.py:273
  6.2 0.7 %collective-permute-start.3 = (bf16[40,1792]{1,0:T(8,128)(2,1)S(1)}, bf16[40,1792]{1,0:T(8,128)(2,1)S(1)}, u32[]{:S(2)}, u32[]{:S(2)}) collective-permute-start(bf16[40,1792]{1,0:T(8,128)(2,1)S(1)} %get-tuple-element.30.refs_0_), channel_id=1, source_target_pairs={{0,0},{1,9},{2,2},{3,11},{4,4},{5,13},{6,6},{7,15},{8,8},{9,1},{10... | collective-permute-start | bytes 430088 | tf_op jit(solution)/shard_map/ppermute | solution.py:273
  6.8 9.5 %fetch.1 = (bf16[16,3584,128]{2,1,0:T(8,128)(2,1)S(1)}, bf16[16,3584,128]{2,1,0:T(8,128)(2,1)S(1)}) custom-call(bf16[40,1792]{1,0:T(8,128)(2,1)S(1)} %get-tuple-element.30.refs_0_, bf16[16,3584,128]{2,1,0:T(8,128)(2,1)} %refs_1_.1, bf16[16,3584,128]{2,1,0:T(8,128)(2,1)} %refs_2_.1), custom_call_target="tpu_custom_call" | custom-call | bytes 29360128 | tf_op jit(solution)/shard_map/fetch/pallas_call | solution.py:297
  16.4 4.7 %collective-permute-start.4 = (bf16[40,1792]{1,0:T(8,128)(2,1)S(1)}, bf16[40,1792]{1,0:T(8,128)(2,1)S(1)}, u32[]{:S(2)}, u32[]{:S(2)}) collective-permute-start(bf16[40,1792]{1,0:T(8,128)(2,1)S(1)} %collective-permute-done.refs_0_), channel_id=1, source_target_pairs={{0,1},{1,0},{2,3},{3,2},{4,5},{5,4},{6,7},{7,6},{8,9},{9,8},{10,11... | collective-permute-start | bytes 430088 | tf_op jit(solution)/shard_map/ppermute | solution.py:22
  21.1 0.4 collective-permute-start.6
  21.7 0.4 collective-permute-done.4.refs_4_
  22.1 0.4 collective-permute-done.5.refs_5_
  22.6 0.3 collective-permute-done.7.refs_7_
  22.9 9.6 %experts.1 = (f32[80,3584]{1,0:T(8,128)S(1)}, bf16[80,3584]{1,0:T(8,128)(2,1)S(1)}) custom-call(bf16[40,1792]{1,0:T(8,128)(2,1)S(1)} %collective-permute-done.refs_0_, bf16[40,1792]{1,0:T(8,128)(2,1)S(1)} %collective-permute-done.1.refs_1_, bf16[40,1792]{1,0:T(8,128)(2,1)S(1)} %collective-permute-done.2.refs_2_, ...), custom_call_target="tpu_custom_call" | custom-call | tf_op jit(solution)/shard_map/experts/pallas_call | solution.py:313
  32.8 1.8 %collective-permute-done.8.got_ref = bf16[80,3584]{1,0:T(8,128)(2,1)S(1)} collective-permute-done((bf16[80,3584]{1,0:T(8,128)(2,1)S(1)}, bf16[80,3584]{1,0:T(8,128)(2,1)S(1)}, u32[]{:S(2)}, u32[]{:S(2)}) %collective-permute-start.8) | collective-permute-done | bytes 573472 | tf_op jit(solution)/shard_map/ppermute | solution.py:22
  34.6 0.3 sum_cores.1
  34.9 1.5 %collective-permute-start.9 = (bf16[40,1792]{1,0:T(8,128)(2,1)S(1)}, bf16[40,1792]{1,0:T(8,128)(2,1)S(1)}, u32[]{:S(2)}, u32[]{:S(2)}) collective-permute-start(bf16[40,1792]{1,0:T(8,128)(2,1)S(1)} %get-tuple-element.41), channel_id=1, source_target_pairs={{0,4},{1,13},{2,6},{3,15},{4,0},{5,9},{6,2},{7,11},{8,12},{9,5},{1... | collective-permute-start | bytes 430088 | tf_op jit(solution)/shard_map/ppermute | solution.py:273
  36.4 1.5 %collective-permute-start.10 = (bf16[40,1792]{1,0:T(8,128)(2,1)S(1)}, bf16[40,1792]{1,0:T(8,128)(2,1)S(1)}, u32[]{:S(2)}, u32[]{:S(2)}) collective-permute-start(bf16[40,1792]{1,0:T(8,128)(2,1)S(1)} %get-tuple-element.42), channel_id=1, source_target_pairs={{0,6},{1,15},{2,4},{3,13},{4,2},{5,11},{6,0},{7,9},{8,14},{9,7},{1... | collective-permute-start | bytes 430088 | tf_op jit(solution)/shard_map/ppermute | solution.py:273
  37.9 0.5 %collective-permute-start.11 = (bf16[40,1792]{1,0:T(8,128)(2,1)S(1)}, bf16[40,1792]{1,0:T(8,128)(2,1)S(1)}, u32[]{:S(2)}, u32[]{:S(2)}) collective-permute-start(bf16[40,1792]{1,0:T(8,128)(2,1)S(1)} %get-tuple-element.43), channel_id=1, source_target_pairs={{0,2},{1,11},{2,0},{3,9},{4,6},{5,15},{6,4},{7,13},{8,10},{9,3},{1... | collective-permute-start | bytes 430088 | tf_op jit(solution)/shard_map/ppermute | solution.py:273
  38.4 0.7 %collective-permute-start.12 = (bf16[40,1792]{1,0:T(8,128)(2,1)S(1)}, bf16[40,1792]{1,0:T(8,128)(2,1)S(1)}, u32[]{:S(2)}, u32[]{:S(2)}) collective-permute-start(bf16[40,1792]{1,0:T(8,128)(2,1)S(1)} %get-tuple-element.44), channel_id=1, source_target_pairs={{0,0},{1,9},{2,2},{3,11},{4,4},{5,13},{6,6},{7,15},{8,8},{9,1},{10... | collective-permute-start | bytes 430088 | tf_op jit(solution)/shard_map/ppermute | solution.py:273
  39.1 1.8 %collective-permute-done.9.refs_0_ = bf16[40,1792]{1,0:T(8,128)(2,1)S(1)} collective-permute-done((bf16[40,1792]{1,0:T(8,128)(2,1)S(1)}, bf16[40,1792]{1,0:T(8,128)(2,1)S(1)}, u32[]{:S(2)}, u32[]{:S(2)}) %collective-permute-start.9) | collective-permute-done | bytes 143392 | tf_op jit(solution)/shard_map/ppermute | solution.py:273
  40.9 3.7 %collective-permute-done.10.refs_1_ = bf16[40,1792]{1,0:T(8,128)(2,1)S(1)} collective-permute-done((bf16[40,1792]{1,0:T(8,128)(2,1)S(1)}, bf16[40,1792]{1,0:T(8,128)(2,1)S(1)}, u32[]{:S(2)}, u32[]{:S(2)}) %collective-permute-start.10) | collective-permute-done | bytes 143392 | tf_op jit(solution)/shard_map/ppermute | solution.py:273
  44.5 2.6 %collective-permute-done.11.refs_2_ = bf16[40,1792]{1,0:T(8,128)(2,1)S(1)} collective-permute-done((bf16[40,1792]{1,0:T(8,128)(2,1)S(1)}, bf16[40,1792]{1,0:T(8,128)(2,1)S(1)}, u32[]{:S(2)}, u32[]{:S(2)}) %collective-permute-start.11) | collective-permute-done | bytes 143392 | tf_op jit(solution)/shard_map/ppermute | solution.py:273
  47.2 0.5 combine.1
  47.7 3.6 %collective-permute-start.13 = (bf16[64,1792]{1,0:T(8,128)(2,1)S(1)}, bf16[64,1792]{1,0:T(8,128)(2,1)S(1)}, u32[]{:S(2)}, u32[]{:S(2)}) collective-permute-start(bf16[64,1792]{1,0:T(8,128)(2,1)S(1)} %get-tuple-element.46), channel_id=1, source_target_pairs={{0,1},{1,0},{2,3},{3,2},{4,5},{5,4},{6,7},{7,6},{8,9},{9,8},{10,11... | collective-permute-start | bytes 688136 | tf_op jit(solution)/shard_map/ppermute | solution.py:22
  51.3 1.1 %collective-permute-done.13 = bf16[64,1792]{1,0:T(8,128)(2,1)S(1)} collective-permute-done((bf16[64,1792]{1,0:T(8,128)(2,1)S(1)}, bf16[64,1792]{1,0:T(8,128)(2,1)S(1)}, u32[]{:S(2)}, u32[]{:S(2)}) %collective-permute-start.13) | collective-permute-done | bytes 229408 | tf_op jit(solution)/shard_map/ppermute | solution.py:22
  52.4 0.7 %add_convert_fusion = bf16[64,1792]{1,0:T(8,128)(2,1)} fusion(f32[64,1792]{1,0:T(8,128)S(1)} %get-tuple-element.45, bf16[64,1792]{1,0:T(8,128)(2,1)S(1)} %collective-permute-done.13), kind=kLoop, calls=%fused_computation | loop fusion | flops 344064 | bytes 917504 | tf_op jit(solution)/shard_map/convert_element_type | solution.py:353
  (12 shorter events, 0.8 us)
Async XLA Ops:
  1.5 14.8 %collective-permute-start = (bf16[40,1792]{1,0:T(8,128)(2,1)S(1)}, bf16[40,1792]{1,0:T(8,128)(2,1)S(1)}, u32[]{:S(2)}, u32[]{:S(2)}) collective-permute-start(bf16[40,1792]{1,0:T(8,128)(2,1)S(1)} %get-tuple-element.27), channel_id=1, source_target_pairs={{0,4},{1,13},{2,6},{3,15},{4,0},{5,9},{6,2},{7,11},{8,12},{9,5},{1... | collective-permute-start | bytes 430088 | tf_op jit(solution)/shard_map/ppermute | solution.py:273
  4.6 11.7 %collective-permute-start.1 = (bf16[40,1792]{1,0:T(8,128)(2,1)S(1)}, bf16[40,1792]{1,0:T(8,128)(2,1)S(1)}, u32[]{:S(2)}, u32[]{:S(2)}) collective-permute-start(bf16[40,1792]{1,0:T(8,128)(2,1)S(1)} %get-tuple-element.28), channel_id=1, source_target_pairs={{0,6},{1,15},{2,4},{3,13},{4,2},{5,11},{6,0},{7,9},{8,14},{9,7},{1... | collective-permute-start | bytes 430088 | tf_op jit(solution)/shard_map/ppermute | solution.py:273
  6.0 10.4 %collective-permute-start.2 = (bf16[40,1792]{1,0:T(8,128)(2,1)S(1)}, bf16[40,1792]{1,0:T(8,128)(2,1)S(1)}, u32[]{:S(2)}, u32[]{:S(2)}) collective-permute-start(bf16[40,1792]{1,0:T(8,128)(2,1)S(1)} %get-tuple-element.29), channel_id=1, source_target_pairs={{0,2},{1,11},{2,0},{3,9},{4,6},{5,15},{6,4},{7,13},{8,10},{9,3},{1... | collective-permute-start | bytes 430088 | tf_op jit(solution)/shard_map/ppermute | solution.py:273
  6.2 10.2 %collective-permute-start.3 = (bf16[40,1792]{1,0:T(8,128)(2,1)S(1)}, bf16[40,1792]{1,0:T(8,128)(2,1)S(1)}, u32[]{:S(2)}, u32[]{:S(2)}) collective-permute-start(bf16[40,1792]{1,0:T(8,128)(2,1)S(1)} %get-tuple-element.30.refs_0_), channel_id=1, source_target_pairs={{0,0},{1,9},{2,2},{3,11},{4,4},{5,13},{6,6},{7,15},{8,8},{9,1},{10... | collective-permute-start | bytes 430088 | tf_op jit(solution)/shard_map/ppermute | solution.py:273
  16.4 30.8 %copy-start = (f32[64,2]{0,1:T(2,128)S(1)}, f32[64,2]{0,1:T(2,128)}, u32[]{:S(2)}) copy-start(f32[64,2]{0,1:T(2,128)} %param.9) | copy-start | bytes 1540
  16.4 5.7 %collective-permute-start.4 = (bf16[40,1792]{1,0:T(8,128)(2,1)S(1)}, bf16[40,1792]{1,0:T(8,128)(2,1)S(1)}, u32[]{:S(2)}, u32[]{:S(2)}) collective-permute-start(bf16[40,1792]{1,0:T(8,128)(2,1)S(1)} %collective-permute-done.refs_0_), channel_id=1, source_target_pairs={{0,1},{1,0},{2,3},{3,2},{4,5},{5,4},{6,7},{7,6},{8,9},{9,8},{10,11... | collective-permute-start | bytes 430088 | tf_op jit(solution)/shard_map/ppermute | solution.py:22
  21.1 1.4 %collective-permute-start.5 = (bf16[40,1792]{1,0:T(8,128)(2,1)S(1)}, bf16[40,1792]{1,0:T(8,128)(2,1)S(1)}, u32[]{:S(2)}, u32[]{:S(2)}) collective-permute-start(bf16[40,1792]{1,0:T(8,128)(2,1)S(1)} %collective-permute-done.1.refs_1_), channel_id=1, source_target_pairs={{0,1},{1,0},{2,3},{3,2},{4,5},{5,4},{6,7},{7,6},{8,9},{9,8},{10,11... | collective-permute-start | bytes 430088 | tf_op jit(solution)/shard_map/ppermute | solution.py:22
  21.1 1.5 %collective-permute-start.6 = (bf16[40,1792]{1,0:T(8,128)(2,1)S(1)}, bf16[40,1792]{1,0:T(8,128)(2,1)S(1)}, u32[]{:S(2)}, u32[]{:S(2)}) collective-permute-start(bf16[40,1792]{1,0:T(8,128)(2,1)S(1)} %collective-permute-done.2.refs_2_), channel_id=1, source_target_pairs={{0,1},{1,0},{2,3},{3,2},{4,5},{5,4},{6,7},{7,6},{8,9},{9,8},{10,11... | collective-permute-start | bytes 430088 | tf_op jit(solution)/shard_map/ppermute | solution.py:22
  21.6 1.4 %collective-permute-start.7 = (bf16[40,1792]{1,0:T(8,128)(2,1)S(1)}, bf16[40,1792]{1,0:T(8,128)(2,1)S(1)}, u32[]{:S(2)}, u32[]{:S(2)}) collective-permute-start(bf16[40,1792]{1,0:T(8,128)(2,1)S(1)} %collective-permute-done.3.refs_3_), channel_id=1, source_target_pairs={{0,1},{1,0},{2,3},{3,2},{4,5},{5,4},{6,7},{7,6},{8,9},{9,8},{10,11... | collective-permute-start | bytes 430088 | tf_op jit(solution)/shard_map/ppermute | solution.py:22
  32.5 2.0 %collective-permute-start.8 = (bf16[80,3584]{1,0:T(8,128)(2,1)S(1)}, bf16[80,3584]{1,0:T(8,128)(2,1)S(1)}, u32[]{:S(2)}, u32[]{:S(2)}) collective-permute-start(bf16[80,3584]{1,0:T(8,128)(2,1)S(1)} %get-tuple-element.40), channel_id=1, source_target_pairs={{0,1},{1,0},{2,3},{3,2},{4,5},{5,4},{6,7},{7,6},{8,9},{9,8},{10,11... | collective-permute-start | bytes 1720328 | tf_op jit(solution)/shard_map/ppermute | solution.py:22
  34.9 6.0 %collective-permute-start.9 = (bf16[40,1792]{1,0:T(8,128)(2,1)S(1)}, bf16[40,1792]{1,0:T(8,128)(2,1)S(1)}, u32[]{:S(2)}, u32[]{:S(2)}) collective-permute-start(bf16[40,1792]{1,0:T(8,128)(2,1)S(1)} %get-tuple-element.41), channel_id=1, source_target_pairs={{0,4},{1,13},{2,6},{3,15},{4,0},{5,9},{6,2},{7,11},{8,12},{9,5},{1... | collective-permute-start | bytes 430088 | tf_op jit(solution)/shard_map/ppermute | solution.py:273
  36.4 8.2 %collective-permute-start.10 = (bf16[40,1792]{1,0:T(8,128)(2,1)S(1)}, bf16[40,1792]{1,0:T(8,128)(2,1)S(1)}, u32[]{:S(2)}, u32[]{:S(2)}) collective-permute-start(bf16[40,1792]{1,0:T(8,128)(2,1)S(1)} %get-tuple-element.42), channel_id=1, source_target_pairs={{0,6},{1,15},{2,4},{3,13},{4,2},{5,11},{6,0},{7,9},{8,14},{9,7},{1... | collective-permute-start | bytes 430088 | tf_op jit(solution)/shard_map/ppermute | solution.py:273
  37.9 9.2 %collective-permute-start.11 = (bf16[40,1792]{1,0:T(8,128)(2,1)S(1)}, bf16[40,1792]{1,0:T(8,128)(2,1)S(1)}, u32[]{:S(2)}, u32[]{:S(2)}) collective-permute-start(bf16[40,1792]{1,0:T(8,128)(2,1)S(1)} %get-tuple-element.43), channel_id=1, source_target_pairs={{0,2},{1,11},{2,0},{3,9},{4,6},{5,15},{6,4},{7,13},{8,10},{9,3},{1... | collective-permute-start | bytes 430088 | tf_op jit(solution)/shard_map/ppermute | solution.py:273
  38.4 8.7 %collective-permute-start.12 = (bf16[40,1792]{1,0:T(8,128)(2,1)S(1)}, bf16[40,1792]{1,0:T(8,128)(2,1)S(1)}, u32[]{:S(2)}, u32[]{:S(2)}) collective-permute-start(bf16[40,1792]{1,0:T(8,128)(2,1)S(1)} %get-tuple-element.44), channel_id=1, source_target_pairs={{0,0},{1,9},{2,2},{3,11},{4,4},{5,13},{6,6},{7,15},{8,8},{9,1},{10... | collective-permute-start | bytes 430088 | tf_op jit(solution)/shard_map/ppermute | solution.py:273
  47.7 4.7 %collective-permute-start.13 = (bf16[64,1792]{1,0:T(8,128)(2,1)S(1)}, bf16[64,1792]{1,0:T(8,128)(2,1)S(1)}, u32[]{:S(2)}, u32[]{:S(2)}) collective-permute-start(bf16[64,1792]{1,0:T(8,128)(2,1)S(1)} %get-tuple-element.46), channel_id=1, source_target_pairs={{0,1},{1,0},{2,3},{3,2},{4,5},{5,4},{6,7},{7,6},{8,9},{9,8},{10,11... | collective-permute-start | bytes 688136 | tf_op jit(solution)/shard_map/ppermute | solution.py:22

commit v4 on v3

--- a/solution.py
+++ b/solution.py
@@ -11,10 +11,12 @@
 SLOTS = 32
 EXPERTS = 28
 CAP = 5
-UNROLL = 8
+UNROLL = 4
 COLUMNS = 896
-LIMIT = 15
+LIMIT = 26
 RING = 3
+PIECE = 2
+EARLY = 4
 MIB = 1 << 20
 
 
@@ -159,7 +161,7 @@
     loads = []
     for a in range(count):
         source, target = refs[1 + a], refs[1 + count + a]
-        size = source.shape[0] // pieces
+        size = target.shape[0] // pieces
         for i in range(pieces):
             piece = pl.ds(i * size, size)
             loads.append(pltpu.make_async_copy(source.at[piece], target.at[piece], sems.at[a, i]))
@@ -171,13 +173,23 @@
 
 def expert_kernel(slots_dev, bufs, *refs):
     buf_refs = refs[:bufs]
-    gate_ref, up_ref, down_hbm, mine_ref, other_ref, x_ref, hidden_ref, down_ref, sems = refs[bufs:]
+    gate_ref, up_ref, up_hbm, down_hbm, mine_ref, other_ref = refs[bufs : bufs + 6]
+    x_ref, hidden_ref, late_ref, down_ref, late_sems, sems = refs[bufs + 6 :]
+    held = up_ref.shape[0]
     ring, blocks, unit, chunk = down_ref.shape
     chunks = down_hbm.shape[2] // chunk
     loads = []
     for i in range(chunks):
         source = down_hbm.at[:, :, pl.ds(i * chunk, chunk)]
         loads.append(pltpu.make_async_copy(source, down_ref.at[i % ring], sems.at[i]))
+
+    def late(i):
+        part = pl.ds(i * PIECE, PIECE)
+        source = up_hbm.at[pl.ds(held + i * PIECE, PIECE)]
+        return pltpu.make_async_copy(source, late_ref.at[part], late_sems.at[i])
+
+    for i in range((blocks - held) // PIECE):
+        late(i).start()
     for load in loads[:ring]:
         load.start()
     rows = slots_dev * CAP
@@ -194,14 +206,24 @@
     index = iota((total, 1), 0)
     row_slot = quotient(index, CAP) - quotient(index, rows) * slots_dev
 
-    def block(b, carry):
-        both = dot(x_ref[...], jnp.concatenate([gate_ref[b], up_ref[b]], axis=1))
+    def block(b, up):
+        both = dot(x_ref[...], jnp.concatenate([gate_ref[b], up], axis=1))
         gate, upper = both[:, :unit], both[:, unit:]
         value = gate / (1.0 + jnp.exp(-gate)) * upper
         hidden_ref[b] = jnp.where(row_slot == b // HB, value, 0.0).astype(jnp.bfloat16)
+
+    def early_block(b, carry):
+        block(b, up_ref[b])
         return carry
 
-    lax.fori_loop(0, blocks, block, 0, unroll=UNROLL)
+    def late_piece(i, carry):
+        late(i).wait()
+        for j in range(PIECE):
+            block(held + i * PIECE + j, late_ref[i * PIECE + j])
+        return carry
+
+    lax.fori_loop(0, held, early_block, 0, unroll=min(held, UNROLL))
+    lax.fori_loop(0, (blocks - held) // PIECE, late_piece, 0, unroll=min((blocks - held), UNROLL) // PIECE)
     hidden = jnp.concatenate([hidden_ref[b] for b in range(blocks)], axis=1)
     for i in range(chunks):
         cols = slice(i * chunk, (i + 1) * chunk)
@@ -296,7 +318,7 @@
     weights = [w_gate, w_up]
     held = pl.pallas_call(
             fetch_kernel,
-            out_shape=[pltpu.VMEM(w.shape, w.dtype) for w in weights[:2]],
+            out_shape=[pltpu.VMEM((count, *w_gate.shape[1:]), w_gate.dtype) for count in (w_gate.shape[0], EARLY)],
             in_specs=[ANY] + [HBM] * 2,
             out_specs=[ANY] * 2,
             scratch_shapes=[pltpu.SemaphoreType.DMA((2, 4))],
@@ -316,17 +338,19 @@
             jax.ShapeDtypeStruct((total // 2, width), jnp.float32),
             jax.ShapeDtypeStruct((total // 2, width), jnp.bfloat16),
         ],
-        in_specs=[VMEM] * (chips + 2) + [HBM],
+        in_specs=[VMEM] * (chips + 2) + [HBM] * 2,
         out_specs=[VMEM] * 2,
         scratch_shapes=[
             pltpu.VMEM((total, width), jnp.bfloat16),
             pltpu.VMEM((blocks, total, unit), jnp.bfloat16),
+            pltpu.VMEM((blocks - EARLY, width, unit), jnp.bfloat16),
             pltpu.VMEM((RING, blocks, unit, COLUMNS), jnp.bfloat16),
+            pltpu.SemaphoreType.DMA(((blocks - EARLY) // PIECE,)),
             pltpu.SemaphoreType.DMA((width // COLUMNS,)),
         ],
         compiler_params=params(LIMIT),
         name="experts",
-    )(*got, *held, from_hbm(w_down))
+    )(*got, *held, from_hbm(w_up), from_hbm(w_down))
 
     back = pl.pallas_call(
         functools.partial(sum_kernel, rows),

time: 53.3 us -> 51.7 us (0.970)
  waiting for transfers between devices: 12.2 us -> 14.5 us
  Pallas kernels: 21.4 us -> 19.3 us
  starting transfers between devices: 18.7 us -> 16.9 us
    pallas_call x1, Pallas kernels: 9.5 us -> 6.27 us  [shards_paired(): pl.pallas_call(fetch_kernel, out_shape=[pltpu.VMEM((count, *w_gate.shape[...]
    ppermute x8, waiting for transfers between devices: 8.06 us -> 10.3 us  [travel(): lax.ppermute(array, ('expert', 'tensor'), [(2 * i + c, 2 * (i ^ p + round...]
    ppermute x6, starting transfers between devices: 9.17 us -> 7.41 us  [swapped(): lax.ppermute(shard, axis, [(i, i ^ 1 << stride) for i in range(lax.axis_s...]
    pallas_call x1, Pallas kernels: 9.56 us -> 10.7 us  [shards_paired(): pl.pallas_call(functools.partial(expert_kernel, slots_dev, chips), out_sh...]
  transfers between devices with their start and end apart: 14 -> 14, of which waited for: 9 -> 11; matrix products, arithmetic and copies ran while one was open for 0% -> 0% of each run, Pallas kernels for 18% -> 12%
where the time goes in v4:
time: 51.7 us; the launch traced here: 51.5 us
  Pallas kernels  19.3 us (37%)
  starting transfers between devices  16.9 us (33%)
  waiting for transfers between devices  14.5 us (28%)
  other arithmetic  0.74 us (1%)
    pallas_call x1, Pallas kernels, shards_paired(): pl.pallas_call(functools.partial(expert_kernel, slots_dev, chips), out_sh...  10.7 us
    ppermute x8, waiting for transfers between devices, travel(): lax.ppermute(array, ('expert', 'tensor'), [(2 * i + c, 2 * (i ^ p + round...  10.3 us
    ppermute x8, starting transfers between devices, travel(): lax.ppermute(array, ('expert', 'tensor'), [(2 * i + c, 2 * (i ^ p + round...  9.5 us
    ppermute x6, starting transfers between devices, swapped(): lax.ppermute(shard, axis, [(i, i ^ 1 << stride) for i in range(lax.axis_s...  7.41 us
    pallas_call x1, Pallas kernels, shards_paired(): pl.pallas_call(fetch_kernel, out_shape=[pltpu.VMEM((count, *w_gate.shape[...  6.27 us
    ppermute x6, waiting for transfers between devices, swapped(): lax.ppermute(shard, axis, [(i, i ^ 1 << stride) for i in range(lax.axis_s...  4.26 us
    pallas_call x1, Pallas kernels, shards_paired(): pl.pallas_call(functools.partial(pick_kernel, slots_dev), out_shape=[jax....  1.52 us
  transfers between devices with their start and end apart: 14, of which 11 were waited for; matrix products, arithmetic and copies ran while one was open for 0% of the time, Pallas kernels for 12%

profile of v4, /device:TPU:0, one launch (start us, length us, event | category | flops | bytes accessed | tf_op | source)
XLA Modules:
  0.0 51.5 jit_solution(4005393745910350017)
XLA Ops:
  0.0 1.5 %pick_rows.1 = (bf16[2,160,128]{2,1,0:T(8,128)(2,1)S(1)}, bf16[40,1792]{1,0:T(8,128)(2,1)S(1)}, bf16[40,1792]{1,0:T(8,128)(2,1)S(1)}, bf16[40,1792]{1,0:T(8,128)(2,1)S(1)}, bf16[40,1792]{1,0:T(8,128)(2,1)S(1)}) custom-call(s32[1]{0:T(128)} %bitcast.1.key_ref, s32[2,64]{1,0:T(2,128)} %bitcast.6, s32[1,32]{1,0:T(1,128)} %bitcast.7, bf16[64,3584]{1,0:T(8,128)(2,1)} %tok_hbm.1), custom_call_target="tpu_custom_call" | custom-call | tf_op jit(solution)/shard_map/pick_rows/pallas_call | solution.py:303
  1.5 3.1 %collective-permute-start = (bf16[40,1792]{1,0:T(8,128)(2,1)S(1)}, bf16[40,1792]{1,0:T(8,128)(2,1)S(1)}, u32[]{:S(2)}, u32[]{:S(2)}) collective-permute-start(bf16[40,1792]{1,0:T(8,128)(2,1)S(1)} %get-tuple-element.27), channel_id=1, source_target_pairs={{0,4},{1,13},{2,6},{3,15},{4,0},{5,9},{6,2},{7,11},{8,12},{9,5},{1... | collective-permute-start | bytes 430088 | tf_op jit(solution)/shard_map/ppermute | solution.py:295
  4.6 1.4 %collective-permute-start.1 = (bf16[40,1792]{1,0:T(8,128)(2,1)S(1)}, bf16[40,1792]{1,0:T(8,128)(2,1)S(1)}, u32[]{:S(2)}, u32[]{:S(2)}) collective-permute-start(bf16[40,1792]{1,0:T(8,128)(2,1)S(1)} %get-tuple-element.28), channel_id=1, source_target_pairs={{0,6},{1,15},{2,4},{3,13},{4,2},{5,11},{6,0},{7,9},{8,14},{9,7},{1... | collective-permute-start | bytes 430088 | tf_op jit(solution)/shard_map/ppermute | solution.py:295
  6.2 0.7 %collective-permute-start.3 = (bf16[40,1792]{1,0:T(8,128)(2,1)S(1)}, bf16[40,1792]{1,0:T(8,128)(2,1)S(1)}, u32[]{:S(2)}, u32[]{:S(2)}) collective-permute-start(bf16[40,1792]{1,0:T(8,128)(2,1)S(1)} %get-tuple-element.30.refs_0_), channel_id=1, source_target_pairs={{0,0},{1,9},{2,2},{3,11},{4,4},{5,13},{6,6},{7,15},{8,8},{9,1},{10... | collective-permute-start | bytes 430088 | tf_op jit(solution)/shard_map/ppermute | solution.py:295
  6.8 6.3 %fetch.1 = (bf16[16,3584,128]{2,1,0:T(8,128)(2,1)S(1)}, bf16[4,3584,128]{2,1,0:T(8,128)(2,1)S(1)}) custom-call(bf16[40,1792]{1,0:T(8,128)(2,1)S(1)} %get-tuple-element.30.refs_0_, bf16[16,3584,128]{2,1,0:T(8,128)(2,1)} %refs_1_.1, bf16[16,3584,128]{2,1,0:T(8,128)(2,1)} %refs_10_.1), custom_call_target="tpu_custom_call" | custom-call | bytes 29360128 | tf_op jit(solution)/shard_map/fetch/pallas_call | solution.py:319
  13.1 1.7 %collective-permute-done.1.refs_1_ = bf16[40,1792]{1,0:T(8,128)(2,1)S(1)} collective-permute-done((bf16[40,1792]{1,0:T(8,128)(2,1)S(1)}, bf16[40,1792]{1,0:T(8,128)(2,1)S(1)}, u32[]{:S(2)}, u32[]{:S(2)}) %collective-permute-start.1) | collective-permute-done | bytes 143392 | tf_op jit(solution)/shard_map/ppermute | solution.py:295
  14.8 0.4 collective-permute-done.2.refs_2_
  15.2 3.6 %collective-permute-start.4 = (bf16[40,1792]{1,0:T(8,128)(2,1)S(1)}, bf16[40,1792]{1,0:T(8,128)(2,1)S(1)}, u32[]{:S(2)}, u32[]{:S(2)}) collective-permute-start(bf16[40,1792]{1,0:T(8,128)(2,1)S(1)} %collective-permute-done.refs_0_), channel_id=1, source_target_pairs={{0,1},{1,0},{2,3},{3,2},{4,5},{5,4},{6,7},{7,6},{8,9},{9,8},{10,11... | collective-permute-start | bytes 430088 | tf_op jit(solution)/shard_map/ppermute | solution.py:24
  18.8 0.5 collective-permute-start.6
  19.3 0.5 collective-permute-done.4.refs_4_
  19.8 0.4 collective-permute-done.5.refs_5_
  20.6 10.7 %experts.1 = (f32[80,3584]{1,0:T(8,128)S(1)}, bf16[80,3584]{1,0:T(8,128)(2,1)S(1)}) custom-call(bf16[40,1792]{1,0:T(8,128)(2,1)S(1)} %collective-permute-done.refs_0_, bf16[40,1792]{1,0:T(8,128)(2,1)S(1)} %collective-permute-done.1.refs_1_, bf16[40,1792]{1,0:T(8,128)(2,1)S(1)} %collective-permute-done.2.refs_2_, ...), custom_call_target="tpu_custom_call" | custom-call | tf_op jit(solution)/shard_map/experts/pallas_call | solution.py:335
  31.6 1.8 %collective-permute-done.8.got_ref = bf16[80,3584]{1,0:T(8,128)(2,1)S(1)} collective-permute-done((bf16[80,3584]{1,0:T(8,128)(2,1)S(1)}, bf16[80,3584]{1,0:T(8,128)(2,1)S(1)}, u32[]{:S(2)}, u32[]{:S(2)}) %collective-permute-start.8) | collective-permute-done | bytes 573472 | tf_op jit(solution)/shard_map/ppermute | solution.py:24
  33.7 0.6 %collective-permute-start.9 = (bf16[40,1792]{1,0:T(8,128)(2,1)S(1)}, bf16[40,1792]{1,0:T(8,128)(2,1)S(1)}, u32[]{:S(2)}, u32[]{:S(2)}) collective-permute-start(bf16[40,1792]{1,0:T(8,128)(2,1)S(1)} %get-tuple-element.41), channel_id=1, source_target_pairs={{0,4},{1,13},{2,6},{3,15},{4,0},{5,9},{6,2},{7,11},{8,12},{9,5},{1... | collective-permute-start | bytes 430088 | tf_op jit(solution)/shard_map/ppermute | solution.py:295
  34.2 2.3 %collective-permute-start.10 = (bf16[40,1792]{1,0:T(8,128)(2,1)S(1)}, bf16[40,1792]{1,0:T(8,128)(2,1)S(1)}, u32[]{:S(2)}, u32[]{:S(2)}) collective-permute-start(bf16[40,1792]{1,0:T(8,128)(2,1)S(1)} %get-tuple-element.42), channel_id=1, source_target_pairs={{0,6},{1,15},{2,4},{3,13},{4,2},{5,11},{6,0},{7,9},{8,14},{9,7},{1... | collective-permute-start | bytes 430088 | tf_op jit(solution)/shard_map/ppermute | solution.py:295
  36.5 0.7 %collective-permute-start.11 = (bf16[40,1792]{1,0:T(8,128)(2,1)S(1)}, bf16[40,1792]{1,0:T(8,128)(2,1)S(1)}, u32[]{:S(2)}, u32[]{:S(2)}) collective-permute-start(bf16[40,1792]{1,0:T(8,128)(2,1)S(1)} %get-tuple-element.43), channel_id=1, source_target_pairs={{0,2},{1,11},{2,0},{3,9},{4,6},{5,15},{6,4},{7,13},{8,10},{9,3},{1... | collective-permute-start | bytes 430088 | tf_op jit(solution)/shard_map/ppermute | solution.py:295
  37.2 0.7 %collective-permute-start.12 = (bf16[40,1792]{1,0:T(8,128)(2,1)S(1)}, bf16[40,1792]{1,0:T(8,128)(2,1)S(1)}, u32[]{:S(2)}, u32[]{:S(2)}) collective-permute-start(bf16[40,1792]{1,0:T(8,128)(2,1)S(1)} %get-tuple-element.44), channel_id=1, source_target_pairs={{0,0},{1,9},{2,2},{3,11},{4,4},{5,13},{6,6},{7,15},{8,8},{9,1},{10... | collective-permute-start | bytes 430088 | tf_op jit(solution)/shard_map/ppermute | solution.py:295
  37.9 1.4 %collective-permute-done.9.refs_0_ = bf16[40,1792]{1,0:T(8,128)(2,1)S(1)} collective-permute-done((bf16[40,1792]{1,0:T(8,128)(2,1)S(1)}, bf16[40,1792]{1,0:T(8,128)(2,1)S(1)}, u32[]{:S(2)}, u32[]{:S(2)}) %collective-permute-start.9) | collective-permute-done | bytes 143392 | tf_op jit(solution)/shard_map/ppermute | solution.py:295
  39.3 6.4 %collective-permute-done.10.refs_1_ = bf16[40,1792]{1,0:T(8,128)(2,1)S(1)} collective-permute-done((bf16[40,1792]{1,0:T(8,128)(2,1)S(1)}, bf16[40,1792]{1,0:T(8,128)(2,1)S(1)}, u32[]{:S(2)}, u32[]{:S(2)}) %collective-permute-start.10) | collective-permute-done | bytes 143392 | tf_op jit(solution)/shard_map/ppermute | solution.py:295
  45.7 0.4 collective-permute-done.11.refs_2_
  46.1 0.5 combine.1
  46.7 3.0 %collective-permute-start.13 = (bf16[64,1792]{1,0:T(8,128)(2,1)S(1)}, bf16[64,1792]{1,0:T(8,128)(2,1)S(1)}, u32[]{:S(2)}, u32[]{:S(2)}) collective-permute-start(bf16[64,1792]{1,0:T(8,128)(2,1)S(1)} %get-tuple-element.46), channel_id=1, source_target_pairs={{0,1},{1,0},{2,3},{3,2},{4,5},{5,4},{6,7},{7,6},{8,9},{9,8},{10,11... | collective-permute-start | bytes 688136 | tf_op jit(solution)/shard_map/ppermute | solution.py:24
  49.7 1.1 %collective-permute-done.13 = bf16[64,1792]{1,0:T(8,128)(2,1)S(1)} collective-permute-done((bf16[64,1792]{1,0:T(8,128)(2,1)S(1)}, bf16[64,1792]{1,0:T(8,128)(2,1)S(1)}, u32[]{:S(2)}, u32[]{:S(2)}) %collective-permute-start.13) | collective-permute-done | bytes 229408 | tf_op jit(solution)/shard_map/ppermute | solution.py:24
  50.8 0.7 %add_convert_fusion = bf16[64,1792]{1,0:T(8,128)(2,1)} fusion(f32[64,1792]{1,0:T(8,128)S(1)} %get-tuple-element.45, bf16[64,1792]{1,0:T(8,128)(2,1)S(1)} %collective-permute-done.13), kind=kLoop, calls=%fused_computation | loop fusion | flops 344064 | bytes 917504 | tf_op jit(solution)/shard_map/convert_element_type | solution.py:377
  (12 shorter events, 1.3 us)
Async XLA Ops:
  1.5 11.6 %collective-permute-start = (bf16[40,1792]{1,0:T(8,128)(2,1)S(1)}, bf16[40,1792]{1,0:T(8,128)(2,1)S(1)}, u32[]{:S(2)}, u32[]{:S(2)}) collective-permute-start(bf16[40,1792]{1,0:T(8,128)(2,1)S(1)} %get-tuple-element.27), channel_id=1, source_target_pairs={{0,4},{1,13},{2,6},{3,15},{4,0},{5,9},{6,2},{7,11},{8,12},{9,5},{1... | collective-permute-start | bytes 430088 | tf_op jit(solution)/shard_map/ppermute | solution.py:295
  4.6 10.2 %collective-permute-start.1 = (bf16[40,1792]{1,0:T(8,128)(2,1)S(1)}, bf16[40,1792]{1,0:T(8,128)(2,1)S(1)}, u32[]{:S(2)}, u32[]{:S(2)}) collective-permute-start(bf16[40,1792]{1,0:T(8,128)(2,1)S(1)} %get-tuple-element.28), channel_id=1, source_target_pairs={{0,6},{1,15},{2,4},{3,13},{4,2},{5,11},{6,0},{7,9},{8,14},{9,7},{1... | collective-permute-start | bytes 430088 | tf_op jit(solution)/shard_map/ppermute | solution.py:295
  6.0 9.2 %collective-permute-start.2 = (bf16[40,1792]{1,0:T(8,128)(2,1)S(1)}, bf16[40,1792]{1,0:T(8,128)(2,1)S(1)}, u32[]{:S(2)}, u32[]{:S(2)}) collective-permute-start(bf16[40,1792]{1,0:T(8,128)(2,1)S(1)} %get-tuple-element.29), channel_id=1, source_target_pairs={{0,2},{1,11},{2,0},{3,9},{4,6},{5,15},{6,4},{7,13},{8,10},{9,3},{1... | collective-permute-start | bytes 430088 | tf_op jit(solution)/shard_map/ppermute | solution.py:295
  6.2 9.0 %collective-permute-start.3 = (bf16[40,1792]{1,0:T(8,128)(2,1)S(1)}, bf16[40,1792]{1,0:T(8,128)(2,1)S(1)}, u32[]{:S(2)}, u32[]{:S(2)}) collective-permute-start(bf16[40,1792]{1,0:T(8,128)(2,1)S(1)} %get-tuple-element.30.refs_0_), channel_id=1, source_target_pairs={{0,0},{1,9},{2,2},{3,11},{4,4},{5,13},{6,6},{7,15},{8,8},{9,1},{10... | collective-permute-start | bytes 430088 | tf_op jit(solution)/shard_map/ppermute | solution.py:295
  15.2 31.0 %copy-start = (f32[64,2]{0,1:T(2,128)S(1)}, f32[64,2]{0,1:T(2,128)}, u32[]{:S(2)}) copy-start(f32[64,2]{0,1:T(2,128)} %param.9) | copy-start | bytes 1540
  15.2 4.6 %collective-permute-start.4 = (bf16[40,1792]{1,0:T(8,128)(2,1)S(1)}, bf16[40,1792]{1,0:T(8,128)(2,1)S(1)}, u32[]{:S(2)}, u32[]{:S(2)}) collective-permute-start(bf16[40,1792]{1,0:T(8,128)(2,1)S(1)} %collective-permute-done.refs_0_), channel_id=1, source_target_pairs={{0,1},{1,0},{2,3},{3,2},{4,5},{5,4},{6,7},{7,6},{8,9},{9,8},{10,11... | collective-permute-start | bytes 430088 | tf_op jit(solution)/shard_map/ppermute | solution.py:24
  18.8 1.4 %collective-permute-start.5 = (bf16[40,1792]{1,0:T(8,128)(2,1)S(1)}, bf16[40,1792]{1,0:T(8,128)(2,1)S(1)}, u32[]{:S(2)}, u32[]{:S(2)}) collective-permute-start(bf16[40,1792]{1,0:T(8,128)(2,1)S(1)} %collective-permute-done.1.refs_1_), channel_id=1, source_target_pairs={{0,1},{1,0},{2,3},{3,2},{4,5},{5,4},{6,7},{7,6},{8,9},{9,8},{10,11... | collective-permute-start | bytes 430088 | tf_op jit(solution)/shard_map/ppermute | solution.py:24
  18.8 1.6 %collective-permute-start.6 = (bf16[40,1792]{1,0:T(8,128)(2,1)S(1)}, bf16[40,1792]{1,0:T(8,128)(2,1)S(1)}, u32[]{:S(2)}, u32[]{:S(2)}) collective-permute-start(bf16[40,1792]{1,0:T(8,128)(2,1)S(1)} %collective-permute-done.2.refs_2_), channel_id=1, source_target_pairs={{0,1},{1,0},{2,3},{3,2},{4,5},{5,4},{6,7},{7,6},{8,9},{9,8},{10,11... | collective-permute-start | bytes 430088 | tf_op jit(solution)/shard_map/ppermute | solution.py:24
  19.3 1.4 %collective-permute-start.7 = (bf16[40,1792]{1,0:T(8,128)(2,1)S(1)}, bf16[40,1792]{1,0:T(8,128)(2,1)S(1)}, u32[]{:S(2)}, u32[]{:S(2)}) collective-permute-start(bf16[40,1792]{1,0:T(8,128)(2,1)S(1)} %collective-permute-done.3.refs_3_), channel_id=1, source_target_pairs={{0,1},{1,0},{2,3},{3,2},{4,5},{5,4},{6,7},{7,6},{8,9},{9,8},{10,11... | collective-permute-start | bytes 430088 | tf_op jit(solution)/shard_map/ppermute | solution.py:24
  31.3 2.0 %collective-permute-start.8 = (bf16[80,3584]{1,0:T(8,128)(2,1)S(1)}, bf16[80,3584]{1,0:T(8,128)(2,1)S(1)}, u32[]{:S(2)}, u32[]{:S(2)}) collective-permute-start(bf16[80,3584]{1,0:T(8,128)(2,1)S(1)} %get-tuple-element.40), channel_id=1, source_target_pairs={{0,1},{1,0},{2,3},{3,2},{4,5},{5,4},{6,7},{7,6},{8,9},{9,8},{10,11... | collective-permute-start | bytes 1720328 | tf_op jit(solution)/shard_map/ppermute | solution.py:24
  33.7 5.7 %collective-permute-start.9 = (bf16[40,1792]{1,0:T(8,128)(2,1)S(1)}, bf16[40,1792]{1,0:T(8,128)(2,1)S(1)}, u32[]{:S(2)}, u32[]{:S(2)}) collective-permute-start(bf16[40,1792]{1,0:T(8,128)(2,1)S(1)} %get-tuple-element.41), channel_id=1, source_target_pairs={{0,4},{1,13},{2,6},{3,15},{4,0},{5,9},{6,2},{7,11},{8,12},{9,5},{1... | collective-permute-start | bytes 430088 | tf_op jit(solution)/shard_map/ppermute | solution.py:295
  34.2 11.5 %collective-permute-start.10 = (bf16[40,1792]{1,0:T(8,128)(2,1)S(1)}, bf16[40,1792]{1,0:T(8,128)(2,1)S(1)}, u32[]{:S(2)}, u32[]{:S(2)}) collective-permute-start(bf16[40,1792]{1,0:T(8,128)(2,1)S(1)} %get-tuple-element.42), channel_id=1, source_target_pairs={{0,6},{1,15},{2,4},{3,13},{4,2},{5,11},{6,0},{7,9},{8,14},{9,7},{1... | collective-permute-start | bytes 430088 | tf_op jit(solution)/shard_map/ppermute | solution.py:295
  36.5 9.6 %collective-permute-start.11 = (bf16[40,1792]{1,0:T(8,128)(2,1)S(1)}, bf16[40,1792]{1,0:T(8,128)(2,1)S(1)}, u32[]{:S(2)}, u32[]{:S(2)}) collective-permute-start(bf16[40,1792]{1,0:T(8,128)(2,1)S(1)} %get-tuple-element.43), channel_id=1, source_target_pairs={{0,2},{1,11},{2,0},{3,9},{4,6},{5,15},{6,4},{7,13},{8,10},{9,3},{1... | collective-permute-start | bytes 430088 | tf_op jit(solution)/shard_map/ppermute | solution.py:295
  37.2 8.9 %collective-permute-start.12 = (bf16[40,1792]{1,0:T(8,128)(2,1)S(1)}, bf16[40,1792]{1,0:T(8,128)(2,1)S(1)}, u32[]{:S(2)}, u32[]{:S(2)}) collective-permute-start(bf16[40,1792]{1,0:T(8,128)(2,1)S(1)} %get-tuple-element.44), channel_id=1, source_target_pairs={{0,0},{1,9},{2,2},{3,11},{4,4},{5,13},{6,6},{7,15},{8,8},{9,1},{10... | collective-permute-start | bytes 430088 | tf_op jit(solution)/shard_map/ppermute | solution.py:295
  46.7 4.1 %collective-permute-start.13 = (bf16[64,1792]{1,0:T(8,128)(2,1)S(1)}, bf16[64,1792]{1,0:T(8,128)(2,1)S(1)}, u32[]{:S(2)}, u32[]{:S(2)}) collective-permute-start(bf16[64,1792]{1,0:T(8,128)(2,1)S(1)} %get-tuple-element.46), channel_id=1, source_target_pairs={{0,1},{1,0},{2,3},{3,2},{4,5},{5,4},{6,7},{7,6},{8,9},{9,8},{10,11... | collective-permute-start | bytes 688136 | tf_op jit(solution)/shard_map/ppermute | solution.py:24

commit v5 on v4

--- a/solution.py
+++ b/solution.py
@@ -223,7 +223,7 @@
         return carry
 
     lax.fori_loop(0, held, early_block, 0, unroll=min(held, UNROLL))
-    lax.fori_loop(0, (blocks - held) // PIECE, late_piece, 0, unroll=min((blocks - held), UNROLL) // PIECE)
+    lax.fori_loop(0, (blocks - held) // PIECE, late_piece, 0, unroll=3)
     hidden = jnp.concatenate([hidden_ref[b] for b in range(blocks)], axis=1)
     for i in range(chunks):
         cols = slice(i * chunk, (i + 1) * chunk)

time: 51.7 us -> 51.7 us (level)
  no operation moved by 1% of the time
where the time goes in v5:
time: 51.7 us; the launch traced here: 51.6 us
  Pallas kernels  19.3 us (37%)
  starting transfers between devices  17.1 us (33%)
  waiting for transfers between devices  14.4 us (28%)
  other arithmetic  0.74 us (1%)
    pallas_call x1, Pallas kernels, shards_paired(): pl.pallas_call(functools.partial(expert_kernel, slots_dev, chips), out_sh...  10.6 us
    ppermute x8, waiting for transfers between devices, travel(): lax.ppermute(array, ('expert', 'tensor'), [(2 * i + c, 2 * (i ^ p + round...  10.1 us
    ppermute x8, starting transfers between devices, travel(): lax.ppermute(array, ('expert', 'tensor'), [(2 * i + c, 2 * (i ^ p + round...  9.5 us
    ppermute x6, starting transfers between devices, swapped(): lax.ppermute(shard, axis, [(i, i ^ 1 << stride) for i in range(lax.axis_s...  7.6 us
    pallas_call x1, Pallas kernels, shards_paired(): pl.pallas_call(fetch_kernel, out_shape=[pltpu.VMEM((count, *w_gate.shape[...  6.27 us
    ppermute x6, waiting for transfers between devices, swapped(): lax.ppermute(shard, axis, [(i, i ^ 1 << stride) for i in range(lax.axis_s...  4.25 us
    pallas_call x1, Pallas kernels, shards_paired(): pl.pallas_call(functools.partial(pick_kernel, slots_dev), out_shape=[jax....  1.52 us
  transfers between devices with their start and end apart: 14, of which 11 were waited for; matrix products, arithmetic and copies ran while one was open for 0% of the time, Pallas kernels for 12%

profile of v5, /device:TPU:0, one launch (start us, length us, event | category | flops | bytes accessed | tf_op | source)
XLA Modules:
  0.0 51.6 jit_solution(6639683292063030812)
XLA Ops:
  0.0 1.5 %pick_rows.1 = (bf16[2,160,128]{2,1,0:T(8,128)(2,1)S(1)}, bf16[40,1792]{1,0:T(8,128)(2,1)S(1)}, bf16[40,1792]{1,0:T(8,128)(2,1)S(1)}, bf16[40,1792]{1,0:T(8,128)(2,1)S(1)}, bf16[40,1792]{1,0:T(8,128)(2,1)S(1)}) custom-call(s32[1]{0:T(128)} %bitcast.1.key_ref, s32[2,64]{1,0:T(2,128)} %bitcast.6, s32[1,32]{1,0:T(1,128)} %bitcast.7, bf16[64,3584]{1,0:T(8,128)(2,1)} %tok_hbm.1), custom_call_target="tpu_custom_call" | custom-call | tf_op jit(solution)/shard_map/pick_rows/pallas_call | solution.py:303
  1.5 3.1 %collective-permute-start = (bf16[40,1792]{1,0:T(8,128)(2,1)S(1)}, bf16[40,1792]{1,0:T(8,128)(2,1)S(1)}, u32[]{:S(2)}, u32[]{:S(2)}) collective-permute-start(bf16[40,1792]{1,0:T(8,128)(2,1)S(1)} %get-tuple-element.27), channel_id=1, source_target_pairs={{0,4},{1,13},{2,6},{3,15},{4,0},{5,9},{6,2},{7,11},{8,12},{9,5},{1... | collective-permute-start | bytes 430088 | tf_op jit(solution)/shard_map/ppermute | solution.py:295
  4.6 1.4 %collective-permute-start.1 = (bf16[40,1792]{1,0:T(8,128)(2,1)S(1)}, bf16[40,1792]{1,0:T(8,128)(2,1)S(1)}, u32[]{:S(2)}, u32[]{:S(2)}) collective-permute-start(bf16[40,1792]{1,0:T(8,128)(2,1)S(1)} %get-tuple-element.28), channel_id=1, source_target_pairs={{0,6},{1,15},{2,4},{3,13},{4,2},{5,11},{6,0},{7,9},{8,14},{9,7},{1... | collective-permute-start | bytes 430088 | tf_op jit(solution)/shard_map/ppermute | solution.py:295
  6.2 0.7 %collective-permute-start.3 = (bf16[40,1792]{1,0:T(8,128)(2,1)S(1)}, bf16[40,1792]{1,0:T(8,128)(2,1)S(1)}, u32[]{:S(2)}, u32[]{:S(2)}) collective-permute-start(bf16[40,1792]{1,0:T(8,128)(2,1)S(1)} %get-tuple-element.30.refs_0_), channel_id=1, source_target_pairs={{0,0},{1,9},{2,2},{3,11},{4,4},{5,13},{6,6},{7,15},{8,8},{9,1},{10... | collective-permute-start | bytes 430088 | tf_op jit(solution)/shard_map/ppermute | solution.py:295
  6.8 6.3 %fetch.1 = (bf16[16,3584,128]{2,1,0:T(8,128)(2,1)S(1)}, bf16[4,3584,128]{2,1,0:T(8,128)(2,1)S(1)}) custom-call(bf16[40,1792]{1,0:T(8,128)(2,1)S(1)} %get-tuple-element.30.refs_0_, bf16[16,3584,128]{2,1,0:T(8,128)(2,1)} %refs_1_.1, bf16[16,3584,128]{2,1,0:T(8,128)(2,1)} %refs_10_.1), custom_call_target="tpu_custom_call" | custom-call | bytes 29360128 | tf_op jit(solution)/shard_map/fetch/pallas_call | solution.py:319
  13.1 1.7 %collective-permute-done.1.refs_1_ = bf16[40,1792]{1,0:T(8,128)(2,1)S(1)} collective-permute-done((bf16[40,1792]{1,0:T(8,128)(2,1)S(1)}, bf16[40,1792]{1,0:T(8,128)(2,1)S(1)}, u32[]{:S(2)}, u32[]{:S(2)}) %collective-permute-start.1) | collective-permute-done | bytes 143392 | tf_op jit(solution)/shard_map/ppermute | solution.py:295
  14.8 0.4 collective-permute-done.2.refs_2_
  15.2 3.6 %collective-permute-start.4 = (bf16[40,1792]{1,0:T(8,128)(2,1)S(1)}, bf16[40,1792]{1,0:T(8,128)(2,1)S(1)}, u32[]{:S(2)}, u32[]{:S(2)}) collective-permute-start(bf16[40,1792]{1,0:T(8,128)(2,1)S(1)} %collective-permute-done.refs_0_), channel_id=1, source_target_pairs={{0,1},{1,0},{2,3},{3,2},{4,5},{5,4},{6,7},{7,6},{8,9},{9,8},{10,11... | collective-permute-start | bytes 430088 | tf_op jit(solution)/shard_map/ppermute | solution.py:24
  18.8 0.5 collective-permute-start.6
  19.3 0.5 collective-permute-done.4.refs_4_
  19.8 0.4 collective-permute-done.5.refs_5_
  20.6 10.6 %experts.1 = (f32[80,3584]{1,0:T(8,128)S(1)}, bf16[80,3584]{1,0:T(8,128)(2,1)S(1)}) custom-call(bf16[40,1792]{1,0:T(8,128)(2,1)S(1)} %collective-permute-done.refs_0_, bf16[40,1792]{1,0:T(8,128)(2,1)S(1)} %collective-permute-done.1.refs_1_, bf16[40,1792]{1,0:T(8,128)(2,1)S(1)} %collective-permute-done.2.refs_2_, ...), custom_call_target="tpu_custom_call" | custom-call | tf_op jit(solution)/shard_map/experts/pallas_call | solution.py:335
  31.6 1.8 %collective-permute-done.8.got_ref = bf16[80,3584]{1,0:T(8,128)(2,1)S(1)} collective-permute-done((bf16[80,3584]{1,0:T(8,128)(2,1)S(1)}, bf16[80,3584]{1,0:T(8,128)(2,1)S(1)}, u32[]{:S(2)}, u32[]{:S(2)}) %collective-permute-start.8) | collective-permute-done | bytes 573472 | tf_op jit(solution)/shard_map/ppermute | solution.py:24
  33.7 0.6 %collective-permute-start.9 = (bf16[40,1792]{1,0:T(8,128)(2,1)S(1)}, bf16[40,1792]{1,0:T(8,128)(2,1)S(1)}, u32[]{:S(2)}, u32[]{:S(2)}) collective-permute-start(bf16[40,1792]{1,0:T(8,128)(2,1)S(1)} %get-tuple-element.41), channel_id=1, source_target_pairs={{0,4},{1,13},{2,6},{3,15},{4,0},{5,9},{6,2},{7,11},{8,12},{9,5},{1... | collective-permute-start | bytes 430088 | tf_op jit(solution)/shard_map/ppermute | solution.py:295
  34.2 2.3 %collective-permute-start.10 = (bf16[40,1792]{1,0:T(8,128)(2,1)S(1)}, bf16[40,1792]{1,0:T(8,128)(2,1)S(1)}, u32[]{:S(2)}, u32[]{:S(2)}) collective-permute-start(bf16[40,1792]{1,0:T(8,128)(2,1)S(1)} %get-tuple-element.42), channel_id=1, source_target_pairs={{0,6},{1,15},{2,4},{3,13},{4,2},{5,11},{6,0},{7,9},{8,14},{9,7},{1... | collective-permute-start | bytes 430088 | tf_op jit(solution)/shard_map/ppermute | solution.py:295
  36.5 0.7 %collective-permute-start.11 = (bf16[40,1792]{1,0:T(8,128)(2,1)S(1)}, bf16[40,1792]{1,0:T(8,128)(2,1)S(1)}, u32[]{:S(2)}, u32[]{:S(2)}) collective-permute-start(bf16[40,1792]{1,0:T(8,128)(2,1)S(1)} %get-tuple-element.43), channel_id=1, source_target_pairs={{0,2},{1,11},{2,0},{3,9},{4,6},{5,15},{6,4},{7,13},{8,10},{9,3},{1... | collective-permute-start | bytes 430088 | tf_op jit(solution)/shard_map/ppermute | solution.py:295
  37.2 0.7 %collective-permute-start.12 = (bf16[40,1792]{1,0:T(8,128)(2,1)S(1)}, bf16[40,1792]{1,0:T(8,128)(2,1)S(1)}, u32[]{:S(2)}, u32[]{:S(2)}) collective-permute-start(bf16[40,1792]{1,0:T(8,128)(2,1)S(1)} %get-tuple-element.44), channel_id=1, source_target_pairs={{0,0},{1,9},{2,2},{3,11},{4,4},{5,13},{6,6},{7,15},{8,8},{9,1},{10... | collective-permute-start | bytes 430088 | tf_op jit(solution)/shard_map/ppermute | solution.py:295
  37.9 1.4 %collective-permute-done.9.refs_0_ = bf16[40,1792]{1,0:T(8,128)(2,1)S(1)} collective-permute-done((bf16[40,1792]{1,0:T(8,128)(2,1)S(1)}, bf16[40,1792]{1,0:T(8,128)(2,1)S(1)}, u32[]{:S(2)}, u32[]{:S(2)}) %collective-permute-start.9) | collective-permute-done | bytes 143392 | tf_op jit(solution)/shard_map/ppermute | solution.py:295
  39.3 6.2 %collective-permute-done.10.refs_1_ = bf16[40,1792]{1,0:T(8,128)(2,1)S(1)} collective-permute-done((bf16[40,1792]{1,0:T(8,128)(2,1)S(1)}, bf16[40,1792]{1,0:T(8,128)(2,1)S(1)}, u32[]{:S(2)}, u32[]{:S(2)}) %collective-permute-start.10) | collective-permute-done | bytes 143392 | tf_op jit(solution)/shard_map/ppermute | solution.py:295
  45.6 0.4 collective-permute-done.11.refs_2_
  46.0 0.5 combine.1
  46.5 3.2 %collective-permute-start.13 = (bf16[64,1792]{1,0:T(8,128)(2,1)S(1)}, bf16[64,1792]{1,0:T(8,128)(2,1)S(1)}, u32[]{:S(2)}, u32[]{:S(2)}) collective-permute-start(bf16[64,1792]{1,0:T(8,128)(2,1)S(1)} %get-tuple-element.46), channel_id=1, source_target_pairs={{0,1},{1,0},{2,3},{3,2},{4,5},{5,4},{6,7},{7,6},{8,9},{9,8},{10,11... | collective-permute-start | bytes 688136 | tf_op jit(solution)/shard_map/ppermute | solution.py:24
  49.7 1.1 %collective-permute-done.13 = bf16[64,1792]{1,0:T(8,128)(2,1)S(1)} collective-permute-done((bf16[64,1792]{1,0:T(8,128)(2,1)S(1)}, bf16[64,1792]{1,0:T(8,128)(2,1)S(1)}, u32[]{:S(2)}, u32[]{:S(2)}) %collective-permute-start.13) | collective-permute-done | bytes 229408 | tf_op jit(solution)/shard_map/ppermute | solution.py:24
  50.8 0.7 %add_convert_fusion = bf16[64,1792]{1,0:T(8,128)(2,1)} fusion(f32[64,1792]{1,0:T(8,128)S(1)} %get-tuple-element.45, bf16[64,1792]{1,0:T(8,128)(2,1)S(1)} %collective-permute-done.13), kind=kLoop, calls=%fused_computation | loop fusion | flops 344064 | bytes 917504 | tf_op jit(solution)/shard_map/convert_element_type | solution.py:377
  (12 shorter events, 1.3 us)
Async XLA Ops:
  1.5 11.6 %collective-permute-start = (bf16[40,1792]{1,0:T(8,128)(2,1)S(1)}, bf16[40,1792]{1,0:T(8,128)(2,1)S(1)}, u32[]{:S(2)}, u32[]{:S(2)}) collective-permute-start(bf16[40,1792]{1,0:T(8,128)(2,1)S(1)} %get-tuple-element.27), channel_id=1, source_target_pairs={{0,4},{1,13},{2,6},{3,15},{4,0},{5,9},{6,2},{7,11},{8,12},{9,5},{1... | collective-permute-start | bytes 430088 | tf_op jit(solution)/shard_map/ppermute | solution.py:295
  4.6 10.2 %collective-permute-start.1 = (bf16[40,1792]{1,0:T(8,128)(2,1)S(1)}, bf16[40,1792]{1,0:T(8,128)(2,1)S(1)}, u32[]{:S(2)}, u32[]{:S(2)}) collective-permute-start(bf16[40,1792]{1,0:T(8,128)(2,1)S(1)} %get-tuple-element.28), channel_id=1, source_target_pairs={{0,6},{1,15},{2,4},{3,13},{4,2},{5,11},{6,0},{7,9},{8,14},{9,7},{1... | collective-permute-start | bytes 430088 | tf_op jit(solution)/shard_map/ppermute | solution.py:295
  6.0 9.2 %collective-permute-start.2 = (bf16[40,1792]{1,0:T(8,128)(2,1)S(1)}, bf16[40,1792]{1,0:T(8,128)(2,1)S(1)}, u32[]{:S(2)}, u32[]{:S(2)}) collective-permute-start(bf16[40,1792]{1,0:T(8,128)(2,1)S(1)} %get-tuple-element.29), channel_id=1, source_target_pairs={{0,2},{1,11},{2,0},{3,9},{4,6},{5,15},{6,4},{7,13},{8,10},{9,3},{1... | collective-permute-start | bytes 430088 | tf_op jit(solution)/shard_map/ppermute | solution.py:295
  6.2 9.0 %collective-permute-start.3 = (bf16[40,1792]{1,0:T(8,128)(2,1)S(1)}, bf16[40,1792]{1,0:T(8,128)(2,1)S(1)}, u32[]{:S(2)}, u32[]{:S(2)}) collective-permute-start(bf16[40,1792]{1,0:T(8,128)(2,1)S(1)} %get-tuple-element.30.refs_0_), channel_id=1, source_target_pairs={{0,0},{1,9},{2,2},{3,11},{4,4},{5,13},{6,6},{7,15},{8,8},{9,1},{10... | collective-permute-start | bytes 430088 | tf_op jit(solution)/shard_map/ppermute | solution.py:295
  15.2 30.8 %copy-start = (f32[64,2]{0,1:T(2,128)S(1)}, f32[64,2]{0,1:T(2,128)}, u32[]{:S(2)}) copy-start(f32[64,2]{0,1:T(2,128)} %param.9) | copy-start | bytes 1540
  15.2 4.6 %collective-permute-start.4 = (bf16[40,1792]{1,0:T(8,128)(2,1)S(1)}, bf16[40,1792]{1,0:T(8,128)(2,1)S(1)}, u32[]{:S(2)}, u32[]{:S(2)}) collective-permute-start(bf16[40,1792]{1,0:T(8,128)(2,1)S(1)} %collective-permute-done.refs_0_), channel_id=1, source_target_pairs={{0,1},{1,0},{2,3},{3,2},{4,5},{5,4},{6,7},{7,6},{8,9},{9,8},{10,11... | collective-permute-start | bytes 430088 | tf_op jit(solution)/shard_map/ppermute | solution.py:24
  18.8 1.4 %collective-permute-start.5 = (bf16[40,1792]{1,0:T(8,128)(2,1)S(1)}, bf16[40,1792]{1,0:T(8,128)(2,1)S(1)}, u32[]{:S(2)}, u32[]{:S(2)}) collective-permute-start(bf16[40,1792]{1,0:T(8,128)(2,1)S(1)} %collective-permute-done.1.refs_1_), channel_id=1, source_target_pairs={{0,1},{1,0},{2,3},{3,2},{4,5},{5,4},{6,7},{7,6},{8,9},{9,8},{10,11... | collective-permute-start | bytes 430088 | tf_op jit(solution)/shard_map/ppermute | solution.py:24
  18.8 1.6 %collective-permute-start.6 = (bf16[40,1792]{1,0:T(8,128)(2,1)S(1)}, bf16[40,1792]{1,0:T(8,128)(2,1)S(1)}, u32[]{:S(2)}, u32[]{:S(2)}) collective-permute-start(bf16[40,1792]{1,0:T(8,128)(2,1)S(1)} %collective-permute-done.2.refs_2_), channel_id=1, source_target_pairs={{0,1},{1,0},{2,3},{3,2},{4,5},{5,4},{6,7},{7,6},{8,9},{9,8},{10,11... | collective-permute-start | bytes 430088 | tf_op jit(solution)/shard_map/ppermute | solution.py:24
  19.3 1.4 %collective-permute-start.7 = (bf16[40,1792]{1,0:T(8,128)(2,1)S(1)}, bf16[40,1792]{1,0:T(8,128)(2,1)S(1)}, u32[]{:S(2)}, u32[]{:S(2)}) collective-permute-start(bf16[40,1792]{1,0:T(8,128)(2,1)S(1)} %collective-permute-done.3.refs_3_), channel_id=1, source_target_pairs={{0,1},{1,0},{2,3},{3,2},{4,5},{5,4},{6,7},{7,6},{8,9},{9,8},{10,11... | collective-permute-start | bytes 430088 | tf_op jit(solution)/shard_map/ppermute | solution.py:24
  31.3 2.0 %collective-permute-start.8 = (bf16[80,3584]{1,0:T(8,128)(2,1)S(1)}, bf16[80,3584]{1,0:T(8,128)(2,1)S(1)}, u32[]{:S(2)}, u32[]{:S(2)}) collective-permute-start(bf16[80,3584]{1,0:T(8,128)(2,1)S(1)} %get-tuple-element.40), channel_id=1, source_target_pairs={{0,1},{1,0},{2,3},{3,2},{4,5},{5,4},{6,7},{7,6},{8,9},{9,8},{10,11... | collective-permute-start | bytes 1720328 | tf_op jit(solution)/shard_map/ppermute | solution.py:24
  33.7 5.7 %collective-permute-start.9 = (bf16[40,1792]{1,0:T(8,128)(2,1)S(1)}, bf16[40,1792]{1,0:T(8,128)(2,1)S(1)}, u32[]{:S(2)}, u32[]{:S(2)}) collective-permute-start(bf16[40,1792]{1,0:T(8,128)(2,1)S(1)} %get-tuple-element.41), channel_id=1, source_target_pairs={{0,4},{1,13},{2,6},{3,15},{4,0},{5,9},{6,2},{7,11},{8,12},{9,5},{1... | collective-permute-start | bytes 430088 | tf_op jit(solution)/shard_map/ppermute | solution.py:295
  34.2 11.3 %collective-permute-start.10 = (bf16[40,1792]{1,0:T(8,128)(2,1)S(1)}, bf16[40,1792]{1,0:T(8,128)(2,1)S(1)}, u32[]{:S(2)}, u32[]{:S(2)}) collective-permute-start(bf16[40,1792]{1,0:T(8,128)(2,1)S(1)} %get-tuple-element.42), channel_id=1, source_target_pairs={{0,6},{1,15},{2,4},{3,13},{4,2},{5,11},{6,0},{7,9},{8,14},{9,7},{1... | collective-permute-start | bytes 430088 | tf_op jit(solution)/shard_map/ppermute | solution.py:295
  36.5 9.4 %collective-permute-start.11 = (bf16[40,1792]{1,0:T(8,128)(2,1)S(1)}, bf16[40,1792]{1,0:T(8,128)(2,1)S(1)}, u32[]{:S(2)}, u32[]{:S(2)}) collective-permute-start(bf16[40,1792]{1,0:T(8,128)(2,1)S(1)} %get-tuple-element.43), channel_id=1, source_target_pairs={{0,2},{1,11},{2,0},{3,9},{4,6},{5,15},{6,4},{7,13},{8,10},{9,3},{1... | collective-permute-start | bytes 430088 | tf_op jit(solution)/shard_map/ppermute | solution.py:295
  37.2 8.7 %collective-permute-start.12 = (bf16[40,1792]{1,0:T(8,128)(2,1)S(1)}, bf16[40,1792]{1,0:T(8,128)(2,1)S(1)}, u32[]{:S(2)}, u32[]{:S(2)}) collective-permute-start(bf16[40,1792]{1,0:T(8,128)(2,1)S(1)} %get-tuple-element.44), channel_id=1, source_target_pairs={{0,0},{1,9},{2,2},{3,11},{4,4},{5,13},{6,6},{7,15},{8,8},{9,1},{10... | collective-permute-start | bytes 430088 | tf_op jit(solution)/shard_map/ppermute | solution.py:295
  46.5 4.3 %collective-permute-start.13 = (bf16[64,1792]{1,0:T(8,128)(2,1)S(1)}, bf16[64,1792]{1,0:T(8,128)(2,1)S(1)}, u32[]{:S(2)}, u32[]{:S(2)}) collective-permute-start(bf16[64,1792]{1,0:T(8,128)(2,1)S(1)} %get-tuple-element.46), channel_id=1, source_target_pairs={{0,1},{1,0},{2,3},{3,2},{4,5},{5,4},{6,7},{7,6},{8,9},{9,8},{10,11... | collective-permute-start | bytes 688136 | tf_op jit(solution)/shard_map/ppermute | solution.py:24

commit v6 on v5

--- a/solution.py
+++ b/solution.py
@@ -223,7 +223,7 @@
         return carry
 
     lax.fori_loop(0, held, early_block, 0, unroll=min(held, UNROLL))
-    lax.fori_loop(0, (blocks - held) // PIECE, late_piece, 0, unroll=3)
+    lax.fori_loop(0, (blocks - held) // PIECE, late_piece, 0, unroll=1)
     hidden = jnp.concatenate([hidden_ref[b] for b in range(blocks)], axis=1)
     for i in range(chunks):
         cols = slice(i * chunk, (i + 1) * chunk)

time: 51.7 us -> 51.7 us (level)
  no operation moved by 1% of the time
where the time goes in v6:
time: 51.7 us; the launch traced here: 51.5 us
  Pallas kernels  19.3 us (37%)
  starting transfers between devices  16.9 us (33%)
  waiting for transfers between devices  14.5 us (28%)
  other arithmetic  0.74 us (1%)
    pallas_call x1, Pallas kernels, shards_paired(): pl.pallas_call(functools.partial(expert_kernel, slots_dev, chips), out_sh...  10.6 us
    ppermute x8, waiting for transfers between devices, travel(): lax.ppermute(array, ('expert', 'tensor'), [(2 * i + c, 2 * (i ^ p + round...  10.3 us
    ppermute x8, starting transfers between devices, travel(): lax.ppermute(array, ('expert', 'tensor'), [(2 * i + c, 2 * (i ^ p + round...  9.5 us
    ppermute x6, starting transfers between devices, swapped(): lax.ppermute(shard, axis, [(i, i ^ 1 << stride) for i in range(lax.axis_s...  7.41 us
    pallas_call x1, Pallas kernels, shards_paired(): pl.pallas_call(fetch_kernel, out_shape=[pltpu.VMEM((count, *w_gate.shape[...  6.27 us
    ppermute x6, waiting for transfers between devices, swapped(): lax.ppermute(shard, axis, [(i, i ^ 1 << stride) for i in range(lax.axis_s...  4.25 us
    pallas_call x1, Pallas kernels, shards_paired(): pl.pallas_call(functools.partial(pick_kernel, slots_dev), out_shape=[jax....  1.52 us
  transfers between devices with their start and end apart: 14, of which 11 were waited for; matrix products, arithmetic and copies ran while one was open for 0% of the time, Pallas kernels for 12%

profile of v6, /device:TPU:0, one launch (start us, length us, event | category | flops | bytes accessed | tf_op | source)
XLA Modules:
  0.0 51.5 jit_solution(4112173771888560257)
XLA Ops:
  0.0 1.5 %pick_rows.1 = (bf16[2,160,128]{2,1,0:T(8,128)(2,1)S(1)}, bf16[40,1792]{1,0:T(8,128)(2,1)S(1)}, bf16[40,1792]{1,0:T(8,128)(2,1)S(1)}, bf16[40,1792]{1,0:T(8,128)(2,1)S(1)}, bf16[40,1792]{1,0:T(8,128)(2,1)S(1)}) custom-call(s32[1]{0:T(128)} %bitcast.1.key_ref, s32[2,64]{1,0:T(2,128)} %bitcast.6, s32[1,32]{1,0:T(1,128)} %bitcast.7, bf16[64,3584]{1,0:T(8,128)(2,1)} %tok_hbm.1), custom_call_target="tpu_custom_call" | custom-call | tf_op jit(solution)/shard_map/pick_rows/pallas_call | solution.py:303
  1.5 3.1 %collective-permute-start = (bf16[40,1792]{1,0:T(8,128)(2,1)S(1)}, bf16[40,1792]{1,0:T(8,128)(2,1)S(1)}, u32[]{:S(2)}, u32[]{:S(2)}) collective-permute-start(bf16[40,1792]{1,0:T(8,128)(2,1)S(1)} %get-tuple-element.27), channel_id=1, source_target_pairs={{0,4},{1,13},{2,6},{3,15},{4,0},{5,9},{6,2},{7,11},{8,12},{9,5},{1... | collective-permute-start | bytes 430088 | tf_op jit(solution)/shard_map/ppermute | solution.py:295
  4.6 1.4 %collective-permute-start.1 = (bf16[40,1792]{1,0:T(8,128)(2,1)S(1)}, bf16[40,1792]{1,0:T(8,128)(2,1)S(1)}, u32[]{:S(2)}, u32[]{:S(2)}) collective-permute-start(bf16[40,1792]{1,0:T(8,128)(2,1)S(1)} %get-tuple-element.28), channel_id=1, source_target_pairs={{0,6},{1,15},{2,4},{3,13},{4,2},{5,11},{6,0},{7,9},{8,14},{9,7},{1... | collective-permute-start | bytes 430088 | tf_op jit(solution)/shard_map/ppermute | solution.py:295
  6.2 0.7 %collective-permute-start.3 = (bf16[40,1792]{1,0:T(8,128)(2,1)S(1)}, bf16[40,1792]{1,0:T(8,128)(2,1)S(1)}, u32[]{:S(2)}, u32[]{:S(2)}) collective-permute-start(bf16[40,1792]{1,0:T(8,128)(2,1)S(1)} %get-tuple-element.30.refs_0_), channel_id=1, source_target_pairs={{0,0},{1,9},{2,2},{3,11},{4,4},{5,13},{6,6},{7,15},{8,8},{9,1},{10... | collective-permute-start | bytes 430088 | tf_op jit(solution)/shard_map/ppermute | solution.py:295
  6.8 6.3 %fetch.1 = (bf16[16,3584,128]{2,1,0:T(8,128)(2,1)S(1)}, bf16[4,3584,128]{2,1,0:T(8,128)(2,1)S(1)}) custom-call(bf16[40,1792]{1,0:T(8,128)(2,1)S(1)} %get-tuple-element.30.refs_0_, bf16[16,3584,128]{2,1,0:T(8,128)(2,1)} %refs_1_.1, bf16[16,3584,128]{2,1,0:T(8,128)(2,1)} %refs_10_.1), custom_call_target="tpu_custom_call" | custom-call | bytes 29360128 | tf_op jit(solution)/shard_map/fetch/pallas_call | solution.py:319
  13.1 1.7 %collective-permute-done.1.refs_1_ = bf16[40,1792]{1,0:T(8,128)(2,1)S(1)} collective-permute-done((bf16[40,1792]{1,0:T(8,128)(2,1)S(1)}, bf16[40,1792]{1,0:T(8,128)(2,1)S(1)}, u32[]{:S(2)}, u32[]{:S(2)}) %collective-permute-start.1) | collective-permute-done | bytes 143392 | tf_op jit(solution)/shard_map/ppermute | solution.py:295
  14.8 0.4 collective-permute-done.2.refs_2_
  15.2 3.6 %collective-permute-start.4 = (bf16[40,1792]{1,0:T(8,128)(2,1)S(1)}, bf16[40,1792]{1,0:T(8,128)(2,1)S(1)}, u32[]{:S(2)}, u32[]{:S(2)}) collective-permute-start(bf16[40,1792]{1,0:T(8,128)(2,1)S(1)} %collective-permute-done.refs_0_), channel_id=1, source_target_pairs={{0,1},{1,0},{2,3},{3,2},{4,5},{5,4},{6,7},{7,6},{8,9},{9,8},{10,11... | collective-permute-start | bytes 430088 | tf_op jit(solution)/shard_map/ppermute | solution.py:24
  18.8 0.5 collective-permute-start.6
  19.3 0.5 collective-permute-done.4.refs_4_
  19.8 0.4 collective-permute-done.5.refs_5_
  20.6 10.6 %experts.1 = (f32[80,3584]{1,0:T(8,128)S(1)}, bf16[80,3584]{1,0:T(8,128)(2,1)S(1)}) custom-call(bf16[40,1792]{1,0:T(8,128)(2,1)S(1)} %collective-permute-done.refs_0_, bf16[40,1792]{1,0:T(8,128)(2,1)S(1)} %collective-permute-done.1.refs_1_, bf16[40,1792]{1,0:T(8,128)(2,1)S(1)} %collective-permute-done.2.refs_2_, ...), custom_call_target="tpu_custom_call" | custom-call | tf_op jit(solution)/shard_map/experts/pallas_call | solution.py:335
  31.6 1.8 %collective-permute-done.8.got_ref = bf16[80,3584]{1,0:T(8,128)(2,1)S(1)} collective-permute-done((bf16[80,3584]{1,0:T(8,128)(2,1)S(1)}, bf16[80,3584]{1,0:T(8,128)(2,1)S(1)}, u32[]{:S(2)}, u32[]{:S(2)}) %collective-permute-start.8) | collective-permute-done | bytes 573472 | tf_op jit(solution)/shard_map/ppermute | solution.py:24
  33.7 0.6 %collective-permute-start.9 = (bf16[40,1792]{1,0:T(8,128)(2,1)S(1)}, bf16[40,1792]{1,0:T(8,128)(2,1)S(1)}, u32[]{:S(2)}, u32[]{:S(2)}) collective-permute-start(bf16[40,1792]{1,0:T(8,128)(2,1)S(1)} %get-tuple-element.41), channel_id=1, source_target_pairs={{0,4},{1,13},{2,6},{3,15},{4,0},{5,9},{6,2},{7,11},{8,12},{9,5},{1... | collective-permute-start | bytes 430088 | tf_op jit(solution)/shard_map/ppermute | solution.py:295
  34.2 2.3 %collective-permute-start.10 = (bf16[40,1792]{1,0:T(8,128)(2,1)S(1)}, bf16[40,1792]{1,0:T(8,128)(2,1)S(1)}, u32[]{:S(2)}, u32[]{:S(2)}) collective-permute-start(bf16[40,1792]{1,0:T(8,128)(2,1)S(1)} %get-tuple-element.42), channel_id=1, source_target_pairs={{0,6},{1,15},{2,4},{3,13},{4,2},{5,11},{6,0},{7,9},{8,14},{9,7},{1... | collective-permute-start | bytes 430088 | tf_op jit(solution)/shard_map/ppermute | solution.py:295
  36.5 0.7 %collective-permute-start.11 = (bf16[40,1792]{1,0:T(8,128)(2,1)S(1)}, bf16[40,1792]{1,0:T(8,128)(2,1)S(1)}, u32[]{:S(2)}, u32[]{:S(2)}) collective-permute-start(bf16[40,1792]{1,0:T(8,128)(2,1)S(1)} %get-tuple-element.43), channel_id=1, source_target_pairs={{0,2},{1,11},{2,0},{3,9},{4,6},{5,15},{6,4},{7,13},{8,10},{9,3},{1... | collective-permute-start | bytes 430088 | tf_op jit(solution)/shard_map/ppermute | solution.py:295
  37.2 0.7 %collective-permute-start.12 = (bf16[40,1792]{1,0:T(8,128)(2,1)S(1)}, bf16[40,1792]{1,0:T(8,128)(2,1)S(1)}, u32[]{:S(2)}, u32[]{:S(2)}) collective-permute-start(bf16[40,1792]{1,0:T(8,128)(2,1)S(1)} %get-tuple-element.44), channel_id=1, source_target_pairs={{0,0},{1,9},{2,2},{3,11},{4,4},{5,13},{6,6},{7,15},{8,8},{9,1},{10... | collective-permute-start | bytes 430088 | tf_op jit(solution)/shard_map/ppermute | solution.py:295
  37.9 1.4 %collective-permute-done.9.refs_0_ = bf16[40,1792]{1,0:T(8,128)(2,1)S(1)} collective-permute-done((bf16[40,1792]{1,0:T(8,128)(2,1)S(1)}, bf16[40,1792]{1,0:T(8,128)(2,1)S(1)}, u32[]{:S(2)}, u32[]{:S(2)}) %collective-permute-start.9) | collective-permute-done | bytes 143392 | tf_op jit(solution)/shard_map/ppermute | solution.py:295
  39.3 6.3 %collective-permute-done.10.refs_1_ = bf16[40,1792]{1,0:T(8,128)(2,1)S(1)} collective-permute-done((bf16[40,1792]{1,0:T(8,128)(2,1)S(1)}, bf16[40,1792]{1,0:T(8,128)(2,1)S(1)}, u32[]{:S(2)}, u32[]{:S(2)}) %collective-permute-start.10) | collective-permute-done | bytes 143392 | tf_op jit(solution)/shard_map/ppermute | solution.py:295
  45.7 0.4 collective-permute-done.11.refs_2_
  46.1 0.5 %combine.1 = (f32[64,1792]{1,0:T(8,128)S(1)}, bf16[64,1792]{1,0:T(8,128)(2,1)S(1)}) custom-call(s32[1]{0:T(128)} %bitcast.core_ref, bf16[2,160,128]{2,1,0:T(8,128)(2,1)S(1)} %get-tuple-element.26.pick_ref, f32[2,64]{1,0:T(2,128)S(1)} %bitcast.5, bf16[40,1792]{1,0:T(8,128)(2,1)S(1)} %collective-permute-done.9.refs_0_, ...), custom_call_target="tpu_custom_call" | custom-call | tf_op jit(solution)/shard_map/combine/pallas_call | solution.py:365
  46.7 3.0 %collective-permute-start.13 = (bf16[64,1792]{1,0:T(8,128)(2,1)S(1)}, bf16[64,1792]{1,0:T(8,128)(2,1)S(1)}, u32[]{:S(2)}, u32[]{:S(2)}) collective-permute-start(bf16[64,1792]{1,0:T(8,128)(2,1)S(1)} %get-tuple-element.46), channel_id=1, source_target_pairs={{0,1},{1,0},{2,3},{3,2},{4,5},{5,4},{6,7},{7,6},{8,9},{9,8},{10,11... | collective-permute-start | bytes 688136 | tf_op jit(solution)/shard_map/ppermute | solution.py:24
  49.7 1.1 %collective-permute-done.13 = bf16[64,1792]{1,0:T(8,128)(2,1)S(1)} collective-permute-done((bf16[64,1792]{1,0:T(8,128)(2,1)S(1)}, bf16[64,1792]{1,0:T(8,128)(2,1)S(1)}, u32[]{:S(2)}, u32[]{:S(2)}) %collective-permute-start.13) | collective-permute-done | bytes 229408 | tf_op jit(solution)/shard_map/ppermute | solution.py:24
  50.8 0.7 %add_convert_fusion = bf16[64,1792]{1,0:T(8,128)(2,1)} fusion(f32[64,1792]{1,0:T(8,128)S(1)} %get-tuple-element.45, bf16[64,1792]{1,0:T(8,128)(2,1)S(1)} %collective-permute-done.13), kind=kLoop, calls=%fused_computation | loop fusion | flops 344064 | bytes 917504 | tf_op jit(solution)/shard_map/convert_element_type | solution.py:377
  (12 shorter events, 1.3 us)
Async XLA Ops:
  1.5 11.6 %collective-permute-start = (bf16[40,1792]{1,0:T(8,128)(2,1)S(1)}, bf16[40,1792]{1,0:T(8,128)(2,1)S(1)}, u32[]{:S(2)}, u32[]{:S(2)}) collective-permute-start(bf16[40,1792]{1,0:T(8,128)(2,1)S(1)} %get-tuple-element.27), channel_id=1, source_target_pairs={{0,4},{1,13},{2,6},{3,15},{4,0},{5,9},{6,2},{7,11},{8,12},{9,5},{1... | collective-permute-start | bytes 430088 | tf_op jit(solution)/shard_map/ppermute | solution.py:295
  4.6 10.2 %collective-permute-start.1 = (bf16[40,1792]{1,0:T(8,128)(2,1)S(1)}, bf16[40,1792]{1,0:T(8,128)(2,1)S(1)}, u32[]{:S(2)}, u32[]{:S(2)}) collective-permute-start(bf16[40,1792]{1,0:T(8,128)(2,1)S(1)} %get-tuple-element.28), channel_id=1, source_target_pairs={{0,6},{1,15},{2,4},{3,13},{4,2},{5,11},{6,0},{7,9},{8,14},{9,7},{1... | collective-permute-start | bytes 430088 | tf_op jit(solution)/shard_map/ppermute | solution.py:295
  6.0 9.2 %collective-permute-start.2 = (bf16[40,1792]{1,0:T(8,128)(2,1)S(1)}, bf16[40,1792]{1,0:T(8,128)(2,1)S(1)}, u32[]{:S(2)}, u32[]{:S(2)}) collective-permute-start(bf16[40,1792]{1,0:T(8,128)(2,1)S(1)} %get-tuple-element.29), channel_id=1, source_target_pairs={{0,2},{1,11},{2,0},{3,9},{4,6},{5,15},{6,4},{7,13},{8,10},{9,3},{1... | collective-permute-start | bytes 430088 | tf_op jit(solution)/shard_map/ppermute | solution.py:295
  6.2 9.0 %collective-permute-start.3 = (bf16[40,1792]{1,0:T(8,128)(2,1)S(1)}, bf16[40,1792]{1,0:T(8,128)(2,1)S(1)}, u32[]{:S(2)}, u32[]{:S(2)}) collective-permute-start(bf16[40,1792]{1,0:T(8,128)(2,1)S(1)} %get-tuple-element.30.refs_0_), channel_id=1, source_target_pairs={{0,0},{1,9},{2,2},{3,11},{4,4},{5,13},{6,6},{7,15},{8,8},{9,1},{10... | collective-permute-start | bytes 430088 | tf_op jit(solution)/shard_map/ppermute | solution.py:295
  15.2 31.0 %copy-start = (f32[64,2]{0,1:T(2,128)S(1)}, f32[64,2]{0,1:T(2,128)}, u32[]{:S(2)}) copy-start(f32[64,2]{0,1:T(2,128)} %param.9) | copy-start | bytes 1540
  15.2 4.6 %collective-permute-start.4 = (bf16[40,1792]{1,0:T(8,128)(2,1)S(1)}, bf16[40,1792]{1,0:T(8,128)(2,1)S(1)}, u32[]{:S(2)}, u32[]{:S(2)}) collective-permute-start(bf16[40,1792]{1,0:T(8,128)(2,1)S(1)} %collective-permute-done.refs_0_), channel_id=1, source_target_pairs={{0,1},{1,0},{2,3},{3,2},{4,5},{5,4},{6,7},{7,6},{8,9},{9,8},{10,11... | collective-permute-start | bytes 430088 | tf_op jit(solution)/shard_map/ppermute | solution.py:24
  18.8 1.4 %collective-permute-start.5 = (bf16[40,1792]{1,0:T(8,128)(2,1)S(1)}, bf16[40,1792]{1,0:T(8,128)(2,1)S(1)}, u32[]{:S(2)}, u32[]{:S(2)}) collective-permute-start(bf16[40,1792]{1,0:T(8,128)(2,1)S(1)} %collective-permute-done.1.refs_1_), channel_id=1, source_target_pairs={{0,1},{1,0},{2,3},{3,2},{4,5},{5,4},{6,7},{7,6},{8,9},{9,8},{10,11... | collective-permute-start | bytes 430088 | tf_op jit(solution)/shard_map/ppermute | solution.py:24
  18.8 1.6 %collective-permute-start.6 = (bf16[40,1792]{1,0:T(8,128)(2,1)S(1)}, bf16[40,1792]{1,0:T(8,128)(2,1)S(1)}, u32[]{:S(2)}, u32[]{:S(2)}) collective-permute-start(bf16[40,1792]{1,0:T(8,128)(2,1)S(1)} %collective-permute-done.2.refs_2_), channel_id=1, source_target_pairs={{0,1},{1,0},{2,3},{3,2},{4,5},{5,4},{6,7},{7,6},{8,9},{9,8},{10,11... | collective-permute-start | bytes 430088 | tf_op jit(solution)/shard_map/ppermute | solution.py:24
  19.3 1.4 %collective-permute-start.7 = (bf16[40,1792]{1,0:T(8,128)(2,1)S(1)}, bf16[40,1792]{1,0:T(8,128)(2,1)S(1)}, u32[]{:S(2)}, u32[]{:S(2)}) collective-permute-start(bf16[40,1792]{1,0:T(8,128)(2,1)S(1)} %collective-permute-done.3.refs_3_), channel_id=1, source_target_pairs={{0,1},{1,0},{2,3},{3,2},{4,5},{5,4},{6,7},{7,6},{8,9},{9,8},{10,11... | collective-permute-start | bytes 430088 | tf_op jit(solution)/shard_map/ppermute | solution.py:24
  31.3 2.0 %collective-permute-start.8 = (bf16[80,3584]{1,0:T(8,128)(2,1)S(1)}, bf16[80,3584]{1,0:T(8,128)(2,1)S(1)}, u32[]{:S(2)}, u32[]{:S(2)}) collective-permute-start(bf16[80,3584]{1,0:T(8,128)(2,1)S(1)} %get-tuple-element.40), channel_id=1, source_target_pairs={{0,1},{1,0},{2,3},{3,2},{4,5},{5,4},{6,7},{7,6},{8,9},{9,8},{10,11... | collective-permute-start | bytes 1720328 | tf_op jit(solution)/shard_map/ppermute | solution.py:24
  33.7 5.7 %collective-permute-start.9 = (bf16[40,1792]{1,0:T(8,128)(2,1)S(1)}, bf16[40,1792]{1,0:T(8,128)(2,1)S(1)}, u32[]{:S(2)}, u32[]{:S(2)}) collective-permute-start(bf16[40,1792]{1,0:T(8,128)(2,1)S(1)} %get-tuple-element.41), channel_id=1, source_target_pairs={{0,4},{1,13},{2,6},{3,15},{4,0},{5,9},{6,2},{7,11},{8,12},{9,5},{1... | collective-permute-start | bytes 430088 | tf_op jit(solution)/shard_map/ppermute | solution.py:295
  34.2 11.5 %collective-permute-start.10 = (bf16[40,1792]{1,0:T(8,128)(2,1)S(1)}, bf16[40,1792]{1,0:T(8,128)(2,1)S(1)}, u32[]{:S(2)}, u32[]{:S(2)}) collective-permute-start(bf16[40,1792]{1,0:T(8,128)(2,1)S(1)} %get-tuple-element.42), channel_id=1, source_target_pairs={{0,6},{1,15},{2,4},{3,13},{4,2},{5,11},{6,0},{7,9},{8,14},{9,7},{1... | collective-permute-start | bytes 430088 | tf_op jit(solution)/shard_map/ppermute | solution.py:295
  36.5 9.6 %collective-permute-start.11 = (bf16[40,1792]{1,0:T(8,128)(2,1)S(1)}, bf16[40,1792]{1,0:T(8,128)(2,1)S(1)}, u32[]{:S(2)}, u32[]{:S(2)}) collective-permute-start(bf16[40,1792]{1,0:T(8,128)(2,1)S(1)} %get-tuple-element.43), channel_id=1, source_target_pairs={{0,2},{1,11},{2,0},{3,9},{4,6},{5,15},{6,4},{7,13},{8,10},{9,3},{1... | collective-permute-start | bytes 430088 | tf_op jit(solution)/shard_map/ppermute | solution.py:295
  37.2 8.9 %collective-permute-start.12 = (bf16[40,1792]{1,0:T(8,128)(2,1)S(1)}, bf16[40,1792]{1,0:T(8,128)(2,1)S(1)}, u32[]{:S(2)}, u32[]{:S(2)}) collective-permute-start(bf16[40,1792]{1,0:T(8,128)(2,1)S(1)} %get-tuple-element.44), channel_id=1, source_target_pairs={{0,0},{1,9},{2,2},{3,11},{4,4},{5,13},{6,6},{7,15},{8,8},{9,1},{10... | collective-permute-start | bytes 430088 | tf_op jit(solution)/shard_map/ppermute | solution.py:295
  46.7 4.1 %collective-permute-start.13 = (bf16[64,1792]{1,0:T(8,128)(2,1)S(1)}, bf16[64,1792]{1,0:T(8,128)(2,1)S(1)}, u32[]{:S(2)}, u32[]{:S(2)}) collective-permute-start(bf16[64,1792]{1,0:T(8,128)(2,1)S(1)} %get-tuple-element.46), channel_id=1, source_target_pairs={{0,1},{1,0},{2,3},{3,2},{4,5},{5,4},{6,7},{7,6},{8,9},{9,8},{10,11... | collective-permute-start | bytes 688136 | tf_op jit(solution)/shard_map/ppermute | solution.py:24
